TPU v7x, 32 devices: a whole 2x2x4 slice. The times are simulated.
32 devices in a mesh: dp: 16 (over z, y, core), tensor: 2 (over x).
Axes of the slice: x: 2, y: 2, z: 4, core: 2. Of those that a mesh axis runs over, the one named last changes fastest.
Arguments:
- tokens: bfloat16 [576, 32, 768], P('tensor', 'dp'), may hold values from -6 to 6
- valid: int32 [32], P('dp'), may hold values 0 or 1
- cotangent: bfloat16 [576, 32, 768], P('tensor', 'dp'), may hold values from -6 to 6
- row_gain: bfloat16 [2, 2, 768], P(None, None, 'dp'), may hold values from 0.099609375 to 1.8984375
- row_bias: bfloat16 [2, 4, 768], P(None, None, 'dp'), may hold values from -3 to 3
- w_qkv: bfloat16 [2, 768, 3, 768], P(None, 'dp', None, 'tensor'), may hold values from -0.21875 to 0.21875
- qv_bias: bfloat16 [2, 2, 768], P(None, None, 'tensor'), may hold values from -3 to 3
- w_proj: bfloat16 [2, 768, 768], P(None, 'tensor', 'dp'), may hold values from -0.75 to 0.75
- w_fc1: bfloat16 [2, 768, 3072], P(None, 'dp', 'tensor'), may hold values from -0.21875 to 0.21875
- fc1_bias: bfloat16 [2, 3072], P(None, 'tensor'), may hold values from -3 to 3
- w_fc2: bfloat16 [2, 3072, 768], P(None, 'tensor', 'dp'), may hold values from -0.109375 to 0.109375
- rel_table: float32 [2, 24, 529], P(None, 'tensor'), may hold values from -5 to 5
Outputs:
- block_out: bfloat16 [576, 32, 768], P('tensor', 'dp')
- grad_tokens: float32 [576, 32, 768], P('tensor', 'dp')
- grad_row_gain: float32 [2, 2, 768], P(None, None, 'dp')
- grad_row_bias: float32 [2, 4, 768], P(None, None, 'dp')
- grad_w_qkv: float32 [2, 768, 3, 768], P(None, 'dp', None, 'tensor')
- grad_qv_bias: float32 [2, 2, 768], P(None, None, 'tensor')
- grad_w_proj: float32 [2, 768, 768], P(None, 'tensor', 'dp')
- grad_w_fc1: float32 [2, 768, 3072], P(None, 'dp', 'tensor')
- grad_fc1_bias: float32 [2, 3072], P(None, 'tensor')
- grad_w_fc2: float32 [2, 3072, 768], P(None, 'tensor', 'dp')
- grad_rel_table: float32 [2, 24, 529], P(None, 'tensor')
All inputs are finite; a program needn't handle non-finite values. No bound on the sum of `valid` on one device may be relied on, other than what follows from the above.
Results may differ from a plain program's by a relative error of at most 0.02.
Values may be sent and summed in bfloat16 or wider, within the bound.
A program may use at most 256 MiB of HBM per device.

v0:
```python
import jax
import jax.numpy as jnp
from jax import lax
from jax.sharding import PartitionSpec as P

WIN = 12
LAYERS = 2
HDIM = 32
SIDE = 24
SHIFT = 6
RELS = 529


EPSILON = 1e-05
MASK_FILL = -100.0


def layer_norm(values, row_gain, row_shift):
    average = jnp.mean(values, axis=-1, keepdims=True)
    centred = values - average
    variance = jnp.mean(centred * centred, axis=-1, keepdims=True)
    return centred * lax.rsqrt(variance + EPSILON) * row_gain + row_shift


def gelu_exact(values):
    return jax.nn.gelu(values, approximate=False)


def to_windows(rows_data, shifted):
    slot_count = rows_data.shape[1]
    trailing = rows_data.shape[2:]
    image_grid = rows_data.reshape((SIDE, SIDE, slot_count) + trailing)
    if shifted:
        image_grid = jnp.roll(image_grid, (-SHIFT, -SHIFT), axis=(0, 1))
    image_grid = image_grid.reshape((2, WIN, 2, WIN, slot_count) + trailing)
    axes_order = (4, 0, 2, 1, 3) + tuple(range(5, 5 + len(trailing)))
    return jnp.transpose(image_grid, axes_order).reshape((slot_count, 4, WIN * WIN) + trailing)


def from_windows(window_data, shifted):
    slot_count = window_data.shape[0]
    trailing = window_data.shape[3:]
    image_grid = window_data.reshape((slot_count, 2, 2, WIN, WIN) + trailing)
    axes_order = (1, 3, 2, 4, 0) + tuple(range(5, 5 + len(trailing)))
    image_grid = jnp.transpose(image_grid, axes_order).reshape((SIDE, SIDE, slot_count) + trailing)
    if shifted:
        image_grid = jnp.roll(image_grid, (SHIFT, SHIFT), axis=(0, 1))
    return image_grid.reshape((SIDE * SIDE, slot_count) + trailing)


def shift_mask():
    places = jnp.arange(SIDE, dtype=jnp.int32)
    band_of = (places >= SIDE - WIN).astype(jnp.int32) + (places >= SIDE - SHIFT).astype(jnp.int32)
    region = band_of[:, None] * 3 + band_of[None, :]
    region = region.reshape(2, WIN, 2, WIN).transpose(0, 2, 1, 3).reshape(4, WIN * WIN)
    same_region = region[:, :, None] == region[:, None, :]
    return jnp.where(same_region, 0.0, MASK_FILL).astype(jnp.float32)


def offset_table():
    places = jnp.arange(WIN, dtype=jnp.int32)
    targets = jnp.arange(2 * WIN - 1, dtype=jnp.int32)
    offsets = places[:, None] - places[None, :] + WIN - 1
    return (targets[None, None, :] == offsets[:, :, None]).astype(jnp.float32)


def table_bias(table_rows):
    one_hot = offset_table()
    shaped = table_rows.reshape(table_rows.shape[0], 2 * WIN - 1, 2 * WIN - 1)
    spread = jnp.einsum(
        "acr,bds,hrs->habcd", one_hot, one_hot, shaped, precision=lax.Precision.HIGHEST
    )
    return spread.reshape(table_rows.shape[0], WIN * WIN, WIN * WIN)


def table_back(score_sum):
    one_hot = offset_table()
    shaped = score_sum.reshape(score_sum.shape[0], WIN, WIN, WIN, WIN)
    folded = jnp.einsum(
        "acr,bds,habcd->hrs", one_hot, one_hot, shaped, precision=lax.Precision.HIGHEST
    )
    return folded.reshape(score_sum.shape[0], RELS)


def attend_image(pieces, bias_add, scale_factor):
    queries, key_rows, value_rows = pieces
    scores = (
        jnp.einsum("wqhc,wkhc->whqk", queries, key_rows, preferred_element_type=jnp.float32)
        * scale_factor
        + bias_add
    )
    row_top = jnp.max(scores, axis=-1, keepdims=True)
    log_total = row_top + jnp.log(jnp.sum(jnp.exp(scores - row_top), axis=-1, keepdims=True))
    prob_rows = jnp.exp(scores - log_total)
    blended = jnp.einsum(
        "whqk,wkhc->wqhc",
        prob_rows.astype(jnp.bfloat16),
        value_rows,
        preferred_element_type=jnp.float32,
    )
    return (blended.astype(jnp.bfloat16), log_total[..., 0])


def attend_back(pieces, bias_add, scale_factor):
    queries, key_rows, value_rows, log_total, grad_out = pieces
    scores = (
        jnp.einsum("wqhc,wkhc->whqk", queries, key_rows, preferred_element_type=jnp.float32)
        * scale_factor
        + bias_add
    )
    prob_rows = jnp.exp(scores - log_total[..., None])
    prob_low = prob_rows.astype(jnp.bfloat16)
    grad_prob = jnp.einsum(
        "wqhc,wkhc->whqk", grad_out, value_rows, preferred_element_type=jnp.float32
    )
    grad_value = jnp.einsum(
        "whqk,wqhc->wkhc", prob_low, grad_out, preferred_element_type=jnp.float32
    ).astype(jnp.bfloat16)
    grad_score = (
        prob_rows * (grad_prob - jnp.sum(grad_prob * prob_rows, axis=-1, keepdims=True))
    ).astype(jnp.bfloat16)
    grad_query = (
        jnp.einsum("whqk,wkhc->wqhc", grad_score, key_rows, preferred_element_type=jnp.float32)
        * scale_factor
    ).astype(jnp.bfloat16)
    grad_key = (
        jnp.einsum("whqk,wqhc->wkhc", grad_score, queries, preferred_element_type=jnp.float32)
        * scale_factor
    ).astype(jnp.bfloat16)
    score_sum = jnp.sum(grad_score, axis=0, dtype=jnp.float32)
    return (grad_query, grad_key, grad_value, score_sum)


def shards(
    tokens,
    valid,
    cotangent,
    row_gain,
    row_bias,
    w_qkv,
    qv_bias,
    w_proj,
    w_fc1,
    fc1_bias,
    w_fc2,
    rel_table,
):
    slot_count = tokens.shape[1]
    heads_here = rel_table.shape[1]
    head_shape = (slot_count, 4, WIN * WIN, heads_here, HDIM)
    window_shape = (slot_count, 4, WIN * WIN, heads_here * HDIM)
    scale_factor = HDIM ** (-0.5)
    residual = tokens.astype(jnp.float32)
    stored = []
    for layer_index in range(LAYERS):
        shifted = layer_index % 2 == 1
        gain_rows, bias_rows, qkv_full, proj_full, fc1_full, fc2_full = (
            lax.all_gather(row_gain[layer_index], "dp", axis=1, tiled=True),
            lax.all_gather(row_bias[layer_index], "dp", axis=1, tiled=True),
            lax.all_gather(w_qkv[layer_index], "dp", axis=0, tiled=True),
            lax.all_gather(w_proj[layer_index], "dp", axis=1, tiled=True),
            lax.all_gather(w_fc1[layer_index], "dp", axis=0, tiled=True),
            lax.all_gather(w_fc2[layer_index], "dp", axis=1, tiled=True),
        )
        gain_rows = gain_rows.astype(jnp.float32)
        bias_rows = bias_rows.astype(jnp.float32)
        normed, norm_back = jax.vjp(layer_norm, residual, gain_rows[0], bias_rows[0])
        full_normed = lax.all_gather(normed.astype(jnp.bfloat16), "tensor", axis=0, tiled=True)
        projected = jnp.einsum(
            "tsd,dke->tske", full_normed, qkv_full, preferred_element_type=jnp.float32
        )
        pair_bias = qv_bias[layer_index].astype(jnp.float32)
        queries = to_windows(
            (projected[:, :, 0] + pair_bias[0]).astype(jnp.bfloat16), shifted
        ).reshape(head_shape)
        key_rows = to_windows(projected[:, :, 1].astype(jnp.bfloat16), shifted).reshape(head_shape)
        value_rows = to_windows(
            (projected[:, :, 2] + pair_bias[1]).astype(jnp.bfloat16), shifted
        ).reshape(head_shape)
        bias_add = table_bias(rel_table[layer_index])[None]
        if shifted:
            bias_add = bias_add + shift_mask()[:, None]
        blended, log_total = lax.map(
            lambda pieces: attend_image(pieces, bias_add, scale_factor),
            (queries, key_rows, value_rows),
        )
        out_rows = from_windows(blended.reshape(window_shape), shifted)
        attention = lax.psum_scatter(
            jnp.einsum(
                "tse,ed->tsd", out_rows, proj_full, preferred_element_type=jnp.float32
            ).astype(jnp.bfloat16),
            "tensor",
            scatter_dimension=0,
            tiled=True,
        ).astype(jnp.float32)
        residual_mid = residual + attention + bias_rows[1]
        normed_mid, mid_back = jax.vjp(layer_norm, residual_mid, gain_rows[1], bias_rows[2])
        mid_low = normed_mid.astype(jnp.bfloat16)
        fc1_use, fc2_use, fc1_bias_use = (fc1_full, fc2_full, fc1_bias[layer_index])
        mlp_input = lax.all_gather(mid_low, "tensor", axis=0, tiled=True)
        hidden_pre = jnp.einsum(
            "tsd,df->tsf", mlp_input, fc1_use, preferred_element_type=jnp.float32
        ) + fc1_bias_use.astype(jnp.float32)
        activated, gelu_back = jax.vjp(gelu_exact, hidden_pre)
        act_low = activated.astype(jnp.bfloat16)
        mlp_sum = lax.psum_scatter(
            jnp.einsum("tsf,fd->tsd", act_low, fc2_use, preferred_element_type=jnp.float32).astype(
                jnp.bfloat16
            ),
            "tensor",
            scatter_dimension=0,
            tiled=True,
        ).astype(jnp.float32)
        residual = residual_mid + mlp_sum + bias_rows[3]
        stored.append(
            (
                shifted,
                norm_back,
                mid_back,
                gelu_back,
                full_normed,
                queries,
                key_rows,
                value_rows,
                log_total,
                bias_add,
                out_rows,
                mlp_input,
                act_low,
                qkv_full,
                proj_full,
                fc1_use,
                fc2_use,
            )
        )
    valid_rows = valid.astype(jnp.float32)[None, :, None]
    block_out = (residual * valid_rows).astype(jnp.bfloat16)
    grad_stream = cotangent.astype(jnp.float32) * valid_rows
    results = [None] * LAYERS
    for layer_index in reversed(range(LAYERS)):
        (
            shifted,
            norm_back,
            mid_back,
            gelu_back,
            full_normed,
            queries,
            key_rows,
            value_rows,
            log_total,
            bias_add,
            out_rows,
            mlp_input,
            act_low,
            qkv_full,
            proj_full,
            fc1_use,
            fc2_use,
        ) = stored[layer_index]
        grad_bias_last = jnp.sum(grad_stream, axis=(0, 1))
        grad_low = grad_stream.astype(jnp.bfloat16)
        grad_full = lax.all_gather(grad_low, "tensor", axis=0, tiled=True)
        grad_act = jnp.einsum("tsd,fd->tsf", grad_full, fc2_use, preferred_element_type=jnp.float32)
        grad_pre = gelu_back(grad_act)[0].astype(jnp.bfloat16)
        fc2_grad = jnp.einsum("tsf,tsd->fd", act_low, grad_full, preferred_element_type=jnp.float32)
        fc1_grad = jnp.einsum(
            "tsd,tsf->df", mlp_input, grad_pre, preferred_element_type=jnp.float32
        )
        fc1_bias_grad = jnp.sum(grad_pre, axis=(0, 1), dtype=jnp.float32)
        grad_mid = lax.psum_scatter(
            jnp.einsum("tsf,df->tsd", grad_pre, fc1_use, preferred_element_type=jnp.float32).astype(
                jnp.bfloat16
            ),
            "tensor",
            scatter_dimension=0,
            tiled=True,
        ).astype(jnp.float32)
        grad_res, grad_gain_mid, grad_bias_mid = mid_back(grad_mid)
        grad_stream = grad_stream + grad_res
        grad_bias_attn = jnp.sum(grad_stream, axis=(0, 1))
        grad_attn = lax.all_gather(grad_stream.astype(jnp.bfloat16), "tensor", axis=0, tiled=True)
        proj_grad = jnp.einsum(
            "tse,tsd->ed", out_rows, grad_attn, preferred_element_type=jnp.float32
        )
        grad_out = jnp.einsum(
            "tsd,ed->tse", grad_attn, proj_full, preferred_element_type=jnp.float32
        ).astype(jnp.bfloat16)
        grad_out = to_windows(grad_out, shifted).reshape(head_shape)
        grad_query, grad_key, grad_value, score_sums = lax.map(
            lambda pieces: attend_back(pieces, bias_add, scale_factor),
            (queries, key_rows, value_rows, log_total, grad_out),
        )
        table_grad = table_back(jnp.sum(score_sums, axis=0))
        grad_qkv = jnp.stack(
            [
                from_windows(member.reshape(window_shape), shifted)
                for member in (grad_query, grad_key, grad_value)
            ],
            axis=2,
        )
        qv_grad = jnp.stack(
            [
                jnp.sum(grad_qkv[:, :, 0], axis=(0, 1), dtype=jnp.float32),
                jnp.sum(grad_qkv[:, :, 2], axis=(0, 1), dtype=jnp.float32),
            ]
        )
        qkv_grad = jnp.einsum(
            "tsd,tske->dke", full_normed, grad_qkv, preferred_element_type=jnp.float32
        )
        grad_normed = lax.psum_scatter(
            jnp.einsum(
                "tske,dke->tsd", grad_qkv, qkv_full, preferred_element_type=jnp.float32
            ).astype(jnp.bfloat16),
            "tensor",
            scatter_dimension=0,
            tiled=True,
        ).astype(jnp.float32)
        grad_res, grad_gain_first, grad_bias_first = norm_back(grad_normed)
        grad_stream = grad_stream + grad_res
        gain_grads = jnp.stack([grad_gain_first, grad_gain_mid])
        bias_grads = jnp.stack([grad_bias_first, grad_bias_attn, grad_bias_mid, grad_bias_last])
        gain_grads, bias_grads = lax.psum((gain_grads, bias_grads), "tensor")
        shard_grads = (
            lax.psum_scatter(
                gain_grads.astype(jnp.bfloat16), "dp", scatter_dimension=1, tiled=True
            ).astype(jnp.float32),
            lax.psum_scatter(
                bias_grads.astype(jnp.bfloat16), "dp", scatter_dimension=1, tiled=True
            ).astype(jnp.float32),
            lax.psum_scatter(
                qkv_grad.astype(jnp.bfloat16), "dp", scatter_dimension=0, tiled=True
            ).astype(jnp.float32),
            lax.psum_scatter(
                proj_grad.astype(jnp.bfloat16), "dp", scatter_dimension=1, tiled=True
            ).astype(jnp.float32),
            lax.psum_scatter(
                fc1_grad.astype(jnp.bfloat16), "dp", scatter_dimension=0, tiled=True
            ).astype(jnp.float32),
            lax.psum_scatter(
                fc2_grad.astype(jnp.bfloat16), "dp", scatter_dimension=1, tiled=True
            ).astype(jnp.float32),
        )
        small_grads = lax.psum((qv_grad, fc1_bias_grad, table_grad), "dp")
        results[layer_index] = tuple(shard_grads) + tuple(small_grads)
    stacked = [
        jnp.stack([results[which_layer][member] for which_layer in range(LAYERS)])
        for member in range(9)
    ]
    (
        grad_row_gain,
        grad_row_bias,
        grad_w_qkv,
        grad_w_proj,
        grad_w_fc1,
        grad_w_fc2,
        grad_qv_bias,
        grad_fc1_bias,
        grad_rel_table,
    ) = stacked
    return (
        block_out,
        grad_stream,
        grad_row_gain,
        grad_row_bias,
        grad_w_qkv,
        grad_qv_bias,
        grad_w_proj,
        grad_w_fc1,
        grad_fc1_bias,
        grad_w_fc2,
        grad_rel_table,
    )


def solution(mesh):
    return jax.shard_map(
        shards,
        mesh=mesh,
        in_specs=(
            P("tensor", "dp", None),
            P("dp"),
            P("tensor", "dp", None),
            P(None, None, "dp"),
            P(None, None, "dp"),
            P(None, "dp", None, "tensor"),
            P(None, None, "tensor"),
            P(None, "tensor", "dp"),
            P(None, "dp", "tensor"),
            P(None, "tensor"),
            P(None, "tensor", "dp"),
            P(None, "tensor", None),
        ),
        out_specs=(
            P("tensor", "dp", None),
            P("tensor", "dp", None),
            P(None, None, "dp"),
            P(None, None, "dp"),
            P(None, "dp", None, "tensor"),
            P(None, None, "tensor"),
            P(None, "tensor", "dp"),
            P(None, "dp", "tensor"),
            P(None, "tensor"),
            P(None, "tensor", "dp"),
            P(None, "tensor", None),
        ),
        check_vma=False,
    )
```

profile of v0, /device:TPU:0, one launch (start us, length us, event | category | flops | bytes accessed | tf_op | source)
XLA Modules:
  0.0 2043.1 jit_solution(3224365836346634279)
XLA Ops:
  11.5 24.3 %all-gather = bf16[1,2,768]{1,0,2:T(2,128)(2,1)S(1)} all-gather(bf16[1,2,48]{1,0,2:T(2,128)(2,1)S(1)} %copy.448), channel_id=2, replica_groups=mesh['dp'=16,'tensor'=2] {'dp'}, dimensions={2}, use_global_device_ids=true | all-gather | bytes 3264 | tf_op jit(solution)/shard_map/all_gather | solution.py:158
  41.5 18.7 all-gather.1
  60.7 10.8 slice_reduce_fusion.6
  75.5 9.0 convolution_bitcast_fusion.1
  84.4 10.2 broadcast_in_dim_reshape.2
  98.6 21.8 %all-gather.3 = bf16[1,384,768]{1,2,0:T(8,128)(2,1)} all-gather(bf16[1,384,48]{1,2,0:T(8,128)(2,1)S(1)} %get-tuple-element.686), channel_id=5, replica_groups=mesh['dp'=16,'tensor'=2] {'dp'}, dimensions={2}, use_global_device_ids=true | all-gather | bytes 626688 | tf_op jit(solution)/shard_map/all_gather | solution.py:161
  120.4 23.9 %all-gather.43.cloned.1.call-done = bf16[1,768,3,384]{3,1,2,0:T(8,128)(2,1)} async-done(((bf16[1,48,3,384]{3,1,2,0:T(8,128)(2,1)}), bf16[1,768,3,384]{3,1,2,0:T(8,128)(2,1)}) %all-gather.43.cloned.1.call-update) | async-done | bytes 1769488 | tf_op jit(solution)/shard_map/all_gather | solution.py:160
  199.9 15.6 while.58
  216.2 8.2 copy.340
  236.9 26.4 %reduce-scatter.29.cloned.1.call-done = bf16[288,2,768]{2,0,1:T(8,128)(2,1)} async-done(((bf16[576,2,768]{2,0,1:T(8,128)(2,1)}), bf16[288,2,768]{2,0,1:T(8,128)(2,1)}) %reduce-scatter.29.cloned.1.call-update) | async-done | bytes 884752 | tf_op jit(solution)/shard_map/reduce_scatter | solution.py:188
  268.6 40.0 %all-gather.45.cloned.1.call-done = bf16[1,768,1536]{2,1,0:T(8,128)(2,1)} async-done(((bf16[1,48,1536]{2,1,0:T(8,128)(2,1)}), bf16[1,768,1536]{2,1,0:T(8,128)(2,1)}) %all-gather.45.cloned.1.call-update) | async-done | bytes 2359312 | tf_op jit(solution)/shard_map/all_gather | solution.py:162
  308.6 30.3 %all-gather.29.cloned.1.call-done = bf16[576,2,768]{2,0,1:T(8,128)(2,1)} async-done(((bf16[288,2,768]{2,0,1:T(8,128)(2,1)}), bf16[576,2,768]{2,0,1:T(8,128)(2,1)}) %all-gather.29.cloned.1.call-update) | async-done | bytes 1769488 | tf_op jit(solution)/shard_map/all_gather | solution.py:200
  348.9 17.6 multiply_convert_fusion.7
  366.5 17.6 all-gather.47.cloned.1.call-done
  391.9 20.3 all-gather.6
  412.7 18.9 all-gather.7
  436.6 11.0 slice_reduce_fusion
  452.7 9.0 convolution_bitcast_fusion
  461.7 10.4 add.431
  474.6 22.2 %all-gather.9 = bf16[1,384,768]{1,2,0:T(8,128)(2,1)} all-gather(bf16[1,384,48]{1,2,0:T(8,128)(2,1)S(1)} %copy-done.78), channel_id=11, replica_groups=mesh['dp'=16,'tensor'=2] {'dp'}, dimensions={2}, use_global_device_ids=true | all-gather | bytes 626688 | tf_op jit(solution)/shard_map/all_gather | solution.py:161
  557.3 17.2 while.60
  574.5 8.2 copy.360
  599.2 24.8 %reduce-scatter.33.cloned.1.call-done = bf16[288,2,768]{2,0,1:T(8,128)(2,1)} async-done(((bf16[576,2,768]{2,0,1:T(8,128)(2,1)}), bf16[288,2,768]{2,0,1:T(8,128)(2,1)}) %reduce-scatter.33.cloned.1.call-update) | async-done | bytes 884752 | tf_op jit(solution)/shard_map/reduce_scatter | solution.py:188
  632.3 37.1 %all-gather.51.cloned.1.call-done = bf16[1,768,1536]{2,1,0:T(8,128)(2,1)} async-done(((bf16[1,48,1536]{2,1,0:T(8,128)(2,1)}), bf16[1,768,1536]{2,1,0:T(8,128)(2,1)}) %all-gather.51.cloned.1.call-update) | async-done | bytes 2359312 | tf_op jit(solution)/shard_map/all_gather | solution.py:162
  669.4 30.3 %all-gather.33.cloned.1.call-done = bf16[576,2,768]{2,0,1:T(8,128)(2,1)} async-done(((bf16[288,2,768]{2,0,1:T(8,128)(2,1)}), bf16[576,2,768]{2,0,1:T(8,128)(2,1)}) %all-gather.33.cloned.1.call-update) | async-done | bytes 1769488 | tf_op jit(solution)/shard_map/all_gather | solution.py:200
  709.8 17.5 multiply_convert_fusion.6
  730.7 45.2 %all-gather.53.cloned.1.call-done = bf16[1,1536,768]{1,2,0:T(8,128)(2,1)} async-done(((bf16[1,1536,48]{1,2,0:T(8,128)(2,1)}), bf16[1,1536,768]{1,2,0:T(8,128)(2,1)}) %all-gather.53.cloned.1.call-update) | async-done | bytes 2359312 | tf_op jit(solution)/shard_map/all_gather | solution.py:163
  776.0 12.1 convert_reduce_fusion.2
  801.5 19.7 reduce-scatter.37.cloned.1.call-done
  825.8 25.8 %reduce-scatter.35.cloned.1.call-done = bf16[288,2,768]{2,0,1:T(8,128)(2,1)} async-done(((bf16[576,2,768]{2,0,1:T(8,128)(2,1)}), bf16[288,2,768]{2,0,1:T(8,128)(2,1)}) %reduce-scatter.35.cloned.1.call-update) | async-done | bytes 884752 | tf_op jit(solution)/shard_map/reduce_scatter | solution.py:206
  858.0 29.5 %all-gather.37.cloned.1.call-done = bf16[576,2,768]{2,0,1:T(8,128)(2,1)} async-done(((bf16[288,2,768]{2,0,1:T(8,128)(2,1)}), bf16[576,2,768]{2,0,1:T(8,128)(2,1)}) %all-gather.37.cloned.1.call-update) | async-done | bytes 1769488 | tf_op jit(solution)/shard_map/all_gather | solution.py:281
  914.3 51.8 %while.61 = (s32[]{:T(128)}, bf16[2,4,144,12,32]{2,4,3,1,0:T(8,128)(2,1)}, bf16[2,4,144,12,32]{2,4,3,1,0:T(8,128)(2,1)}, bf16[2,4,144,12,32]{2,4,3,1,0:T(8,128)(...) while((s32[]{:T(128)}, ...), condition=%wide.region_26.27_spmd.clone, body=%wide.region_23.26_spmd.clone.sunk | while | flops 331299072 | bytes 80667464 | solution.py:289
  922.0 8.0 convert_reduce_fusion.18
  947.9 8.0 convert_reduce_fusion.18
  966.2 8.2 copy.374
  982.4 7.3 copy.377
  997.6 8.2 copy.380
  1029.6 28.3 %reduce-scatter.39.cloned.1.call-done = bf16[288,2,768]{2,0,1:T(8,128)(2,1)} async-done(((bf16[576,2,768]{2,0,1:T(8,128)(2,1)}), bf16[288,2,768]{2,0,1:T(8,128)(2,1)}) %reduce-scatter.39.cloned.1.call-update) | async-done | bytes 884752 | tf_op jit(solution)/shard_map/reduce_scatter | solution.py:310
  1065.7 29.4 %all-gather.39.cloned.1.call-done = bf16[576,2,768]{2,0,1:T(8,128)(2,1)} async-done(((bf16[288,2,768]{2,0,1:T(8,128)(2,1)}), bf16[576,2,768]{2,0,1:T(8,128)(2,1)}) %all-gather.39.cloned.1.call-update) | async-done | bytes 1769488 | tf_op jit(solution)/shard_map/all_gather | solution.py:262
  1095.0 12.1 convert_reduce_fusion.3
  1113.1 28.3 %reduce-scatter.41.cloned.1.call-done = bf16[288,2,768]{2,0,1:T(8,128)(2,1)} async-done(((bf16[576,2,768]{2,0,1:T(8,128)(2,1)}), bf16[288,2,768]{2,0,1:T(8,128)(2,1)}) %reduce-scatter.41.cloned.1.call-update) | async-done | bytes 884752 | tf_op jit(solution)/shard_map/reduce_scatter | solution.py:270
  1149.5 7.3 bitcast_convert_fusion
  1163.6 7.4 bitcast_convert_fusion.2
  1174.5 10.1 reshape.453
  1184.6 21.4 %copy.431 = f32[12,12,12,12,12]{4,3,1,2,0:T(8,128)} copy(f32[12,12,12,12,12]{2,1,4,3,0:T(8,128)} %reshape.453) | data formatting | bytes 1990656 | tf_op jit(solution)/shard_map/reshape | solution.py:78
  1206.0 14.5 convolution_bitcast_fusion.4
  1253.0 34.3 %while.59 = (s32[]{:T(128)}, bf16[2,4,144,12,32]{2,4,3,1,0:T(8,128)(2,1)}, bf16[2,4,144,12,32]{2,4,3,1,0:T(8,128)(2,1)}, bf16[2,4,144,12,32]{2,4,3,1,0:T(8,128)(...) while((s32[]{:T(128)}, ...), condition=%wide.region_36.37_spmd, body=%wide.region_33.36_spmd.sunk | while | flops 336275712 | bytes 97055088 | solution.py:289
  1287.3 8.2 copy.390
  1302.9 8.2 copy.394
  1322.0 10.1 reshape.452
  1332.2 21.3 %copy.428 = f32[12,12,12,12,12]{4,3,1,2,0:T(8,128)} copy(f32[12,12,12,12,12]{2,1,4,3,0:T(8,128)} %reshape.452) | data formatting | bytes 1990656 | tf_op jit(solution)/shard_map/reshape | solution.py:78
  1353.4 14.6 convolution_bitcast_fusion.5
  1421.6 22.4 %reduce-scatter.53.cloned.1.call-done = bf16[48,1536]{1,0:T(8,128)(2,1)} async-done(((bf16[768,1536]{1,0:T(8,128)(2,1)}), bf16[48,1536]{1,0:T(8,128)(2,1)}) %reduce-scatter.53.cloned.1.call-update) | async-done | bytes 147472 | tf_op jit(solution)/shard_map/reduce_scatter | solution.py:336
  1445.8 89.7 %all-reduce.4.cloned.1.call-done = (f32[1,2,384]{2,1,0:T(2,128)}, f32[1,2,384]{2,1,0:T(2,128)}, f32[1,1536]{1,0:T(1,128)}, f32[1,1536]{1,0:T(1,128)}, f32[1,12,529]{2,1,0:T(8,128)}, /*index=5*/f32[1,12,529]{2,1,0:T(8,128)}) async-done(((f32[1,2,384]{2,1,0:T(2,128)}, f32[1,2,384]{2,1,0:T(2,128)}, f32[1,1536]{1,0:T(1,128)}, f32[1,1536]{1,0:T(1,128)}, f32[1,12,529]{2,1,0:T(8,128)}, ...) | async-done | bytes 69232 | tf_op jit(solution)/shard_map/psum | solution.py:343
  1539.6 57.2 %reduce-scatter.51.cloned.1.call-done = bf16[384,48]{0,1:T(8,128)(2,1)} async-done(((bf16[384,768]{0,1:T(8,128)(2,1)}), bf16[384,48]{0,1:T(8,128)(2,1)}) %reduce-scatter.51.cloned.1.call-update) | async-done | bytes 36880 | tf_op jit(solution)/shard_map/reduce_scatter | solution.py:333
  1596.8 57.4 %reduce-scatter.49.cloned.1.call-done = bf16[384,48]{0,1:T(8,128)(2,1)} async-done(((bf16[384,768]{0,1:T(8,128)(2,1)}), bf16[384,48]{0,1:T(8,128)(2,1)}) %reduce-scatter.49.cloned.1.call-update) | async-done | bytes 36880 | tf_op jit(solution)/shard_map/reduce_scatter | solution.py:333
  1655.7 28.1 %reduce-scatter.43.cloned.1.call-done = bf16[288,2,768]{2,0,1:T(8,128)(2,1)} async-done(((bf16[576,2,768]{2,0,1:T(8,128)(2,1)}), bf16[288,2,768]{2,0,1:T(8,128)(2,1)}) %reduce-scatter.43.cloned.1.call-update) | async-done | bytes 884752 | tf_op jit(solution)/shard_map/reduce_scatter | solution.py:310
  1691.1 8.5 all-reduce.1
  1701.2 46.4 %reduce-scatter.47.cloned.1.call-done = bf16[48,3,384]{2,0,1:T(8,128)(2,1)} async-done(((bf16[768,3,384]{2,0,1:T(8,128)(2,1)}), bf16[48,3,384]{2,0,1:T(8,128)(2,1)}) %reduce-scatter.47.cloned.1.call-update) | async-done | bytes 110608 | tf_op jit(solution)/shard_map/reduce_scatter | solution.py:330
  1747.7 63.0 %reduce-scatter.45.cloned.1.call-done = bf16[48,3,384]{2,0,1:T(8,128)(2,1)} async-done(((bf16[768,3,384]{2,0,1:T(8,128)(2,1)}), bf16[48,3,384]{2,0,1:T(8,128)(2,1)}) %reduce-scatter.45.cloned.1.call-update) | async-done | bytes 110608 | tf_op jit(solution)/shard_map/reduce_scatter | solution.py:330
  1824.4 42.4 %reduce-scatter.61.cloned.1.call-done = bf16[48,2]{1,0:T(8,128)(2,1)} async-done(((bf16[768,2]{1,0:T(8,128)(2,1)}), bf16[48,2]{1,0:T(8,128)(2,1)}) %reduce-scatter.61.cloned.1.call-update) | async-done | bytes 208
  1867.6 55.2 %reduce-scatter.63.cloned.1.call-done = bf16[48,2]{1,0:T(8,128)(2,1)} async-done(((bf16[768,2]{1,0:T(8,128)(2,1)}), bf16[48,2]{1,0:T(8,128)(2,1)}) %reduce-scatter.63.cloned.1.call-update) | async-done | bytes 208
  1924.2 54.7 %reduce-scatter.65.cloned.1.call-done = bf16[48,4]{1,0:T(8,128)(2,1)} async-done(((bf16[768,4]{1,0:T(8,128)(2,1)}), bf16[48,4]{1,0:T(8,128)(2,1)}) %reduce-scatter.65.cloned.1.call-update) | async-done | bytes 400
  1979.7 55.3 %reduce-scatter.67.cloned.1.call-done = bf16[48,4]{1,0:T(8,128)(2,1)} async-done(((bf16[768,4]{1,0:T(8,128)(2,1)}), bf16[48,4]{1,0:T(8,128)(2,1)}) %reduce-scatter.67.cloned.1.call-update) | async-done | bytes 400
  (718 shorter events, 584.1 us)
Async XLA Ops:
  7.2 33.7 %copy-start.134 = (bf16[2,4,48]{2,1,0:T(4,128)(2,1)S(1)}, bf16[2,4,48]{2,1,0:T(4,128)(2,1)}, u32[]{:S(2)}) copy-start(bf16[2,4,48]{2,1,0:T(4,128)(2,1)} %param.24) | copy-start | bytes 2308
  7.2 113.2 %all-gather.27.cloned.1.call-start = ((), (), s32[]{:S(2)}) async-start(), calls=%async_computation.20 | async-start | bytes 2654208 | tf_op jit(solution)/shard_map/all_gather | solution.py:168
  8.6 62.9 %copy-start.81 = (f32[288,2]{0,1:T(2,128)}, f32[288,2]{0,1:T(2,128)S(1)}, u32[]{:S(2)}) copy-start(f32[288,2]{0,1:T(2,128)S(1)} %broadcast_multiply_fusion.3) | copy-start | bytes 6916
  10.2 61.3 %copy-start.95 = (f32[288,2]{0,1:T(2,128)}, f32[288,2]{0,1:T(2,128)S(1)}, u32[]{:S(2)}) copy-start(f32[288,2]{0,1:T(2,128)S(1)} %fusion.237) | copy-start | bytes 6916
  11.5 60.0 %copy-start.3 = (bf16[288,2,768]{2,1,0:T(2,128)(2,1)S(1)}, bf16[288,2,768]{2,1,0:T(2,128)(2,1)}, u32[]{:S(2)}) copy-start(bf16[288,2,768]{2,1,0:T(2,128)(2,1)} %param.20) | copy-start | bytes 2654212
  40.9 32.0 %copy-start.87 = (f32[768]{0:T(1024)}, f32[768]{0:T(1024)S(1)}, u32[]{:S(2)}) copy-start(f32[768]{0:T(1024)S(1)} %get-tuple-element.542) | copy-start | bytes 9220
  40.9 224.6 %copy-start.85 = (f32[768]{0:T(1024)}, f32[768]{0:T(1024)S(1)}, u32[]{:S(2)}) copy-start(f32[768]{0:T(1024)S(1)} %get-tuple-element.543) | copy-start | bytes 9220
  71.5 376.2 %copy-start.74 = (f32[768]{0:T(1024)}, f32[768]{0:T(1024)S(1)}, u32[]{:S(2)}) copy-start(f32[768]{0:T(1024)S(1)} %get-tuple-element.540) | copy-start | bytes 9220
  72.8 71.4 %all-gather.43.cloned.1.call-start = ((), (), s32[]{:S(2)}) async-start(), calls=%async_computation.44 | async-start | bytes 1880064 | tf_op jit(solution)/shard_map/all_gather | solution.py:160
  73.6 189.7 %reduce-scatter.29.cloned.1.call-start = ((), (), s32[]{:S(2)}) async-start(), calls=%async_computation.21 | async-start | bytes 2654208 | tf_op jit(solution)/shard_map/reduce_scatter | solution.py:188
  74.8 377.9 %copy-start.68 = (s32[12,12]{1,0:T(8,128)}, s32[12,12]{1,0:T(8,128)S(1)}, u32[]{:S(2)}) copy-start(s32[12,12]{1,0:T(8,128)S(1)} %subtract_add_fusion) | copy-start | bytes 1732
  236.1 72.5 %all-gather.45.cloned.1.call-start = ((), (), s32[]{:S(2)}) async-start(), calls=%async_computation.45 | async-start | bytes 2506752 | tf_op jit(solution)/shard_map/all_gather | solution.py:162
  236.9 102.0 %all-gather.29.cloned.1.call-start = ((), (), s32[]{:S(2)}) async-start(), calls=%async_computation.22 | async-start | bytes 2654208 | tf_op jit(solution)/shard_map/all_gather | solution.py:200
  265.4 73.5 %copy-start.104 = (f32[288,2]{0,1:T(2,128)}, f32[288,2]{0,1:T(2,128)S(1)}, u32[]{:S(2)}) copy-start(f32[288,2]{0,1:T(2,128)S(1)} %multiply_reduce_fusion.4) | copy-start | bytes 6916
  265.4 73.4 %copy-start.93 = (f32[288,2]{0,1:T(2,128)}, f32[288,2]{0,1:T(2,128)S(1)}, u32[]{:S(2)}) copy-start(f32[288,2]{0,1:T(2,128)S(1)} %fusion.238) | copy-start | bytes 6916
  266.9 117.2 %all-gather.47.cloned.1.call-start = ((), (), s32[]{:S(2)}) async-start(), calls=%async_computation.46 | async-start | bytes 2506752 | tf_op jit(solution)/shard_map/all_gather | solution.py:163
  267.7 180.0 %reduce-scatter.31.cloned.1.call-start = ((), (), s32[]{:S(2)}) async-start(), calls=%async_computation.23 | async-start | bytes 2654208 | tf_op jit(solution)/shard_map/reduce_scatter | solution.py:206
  268.6 77.4 %copy-start.99 = (f32[1536]{0:T(1024)}, f32[1536]{0:T(1024)S(1)}, u32[]{:S(2)}) copy-start(f32[1536]{0:T(1024)S(1)} %get-tuple-element.547) | copy-start | bytes 18436
  391.0 105.8 %all-gather.49.cloned.1.call-start = ((), (), s32[]{:S(2)}) async-start(), calls=%async_computation.47 | async-start | bytes 1880064 | tf_op jit(solution)/shard_map/all_gather | solution.py:160
  391.8 105.0 %all-gather.31.cloned.1.call-start = ((), (), s32[]{:S(2)}) async-start(), calls=%async_computation.24 | async-start | bytes 2654208 | tf_op jit(solution)/shard_map/all_gather | solution.py:168
  391.9 55.7 %copy-start.110 = (f32[768]{0:T(1024)S(1)}, f32[768]{0:T(1024)}, u32[]{:S(2)}) copy-start(f32[768]{0:T(1024)} %get-tuple-element.538) | copy-start | bytes 9220
  451.8 172.2 %reduce-scatter.33.cloned.1.call-start = ((), (), s32[]{:S(2)}) async-start(), calls=%async_computation.25 | async-start | bytes 2654208 | tf_op jit(solution)/shard_map/reduce_scatter | solution.py:188
  598.2 71.2 %all-gather.51.cloned.1.call-start = ((), (), s32[]{:S(2)}) async-start(), calls=%async_computation.48 | async-start | bytes 2506752 | tf_op jit(solution)/shard_map/all_gather | solution.py:162
  599.0 100.7 %all-gather.33.cloned.1.call-start = ((), (), s32[]{:S(2)}) async-start(), calls=%async_computation.26 | async-start | bytes 2654208 | tf_op jit(solution)/shard_map/all_gather | solution.py:200
  628.5 71.2 %copy-start.101 = (f32[1536]{0:T(1024)S(1)}, f32[1536]{0:T(1024)}, u32[]{:S(2)}) copy-start(f32[1536]{0:T(1024)} %get-tuple-element.546) | copy-start | bytes 18436
  628.5 102.2 %all-gather.35.cloned.1.call-start = ((), (), s32[]{:S(2)}) async-start(), calls=%async_computation.28 | async-start | bytes 2654208 | tf_op jit(solution)/shard_map/all_gather | solution.py:262
  631.6 144.3 %all-gather.53.cloned.1.call-start = ((), (), s32[]{:S(2)}) async-start(), calls=%async_computation.49 | async-start | bytes 2506752 | tf_op jit(solution)/shard_map/all_gather | solution.py:163
  632.2 189.0 %reduce-scatter.37.cloned.1.call-start = ((), (), s32[]{:S(2)}) async-start(), calls=%async_computation.29 | async-start | bytes 2654208 | tf_op jit(solution)/shard_map/reduce_scatter | solution.py:270
  794.1 57.5 %reduce-scatter.35.cloned.1.call-start = ((), (), s32[]{:S(2)}) async-start(), calls=%async_computation.27 | async-start | bytes 2654208 | tf_op jit(solution)/shard_map/reduce_scatter | solution.py:206
  801.4 86.0 %all-gather.37.cloned.1.call-start = ((), (), s32[]{:S(2)}) async-start(), calls=%async_computation.30 | async-start | bytes 2654208 | tf_op jit(solution)/shard_map/all_gather | solution.py:281
  857.9 200.0 %reduce-scatter.39.cloned.1.call-start = ((), (), s32[]{:S(2)}) async-start(), calls=%async_computation.31 | async-start | bytes 2654208 | tf_op jit(solution)/shard_map/reduce_scatter | solution.py:310
  1025.8 32.1 %copy-start.84 = (f32[288,2]{0,1:T(2,128)S(1)}, f32[288,2]{0,1:T(2,128)}, u32[]{:S(2)}) copy-start(f32[288,2]{0,1:T(2,128)} %copy-done.83) | copy-start | bytes 6916
  1025.8 32.1 %copy-start.90 = (f32[768]{0:T(1024)S(1)}, f32[768]{0:T(1024)}, u32[]{:S(2)}) copy-start(f32[768]{0:T(1024)} %copy-done.89) | copy-start | bytes 9220
  1029.6 32.4 %copy-start.25 = (f32[288,2,768]{2,0,1:T(8,128)S(1)}, f32[288,2,768]{2,0,1:T(8,128)}, u32[]{:S(2)}) copy-start(f32[288,2,768]{2,0,1:T(8,128)} %copy-done.24) | copy-start | bytes 5308420
  1029.6 65.4 %all-gather.39.cloned.1.call-start = ((), (), s32[]{:S(2)}) async-start(), calls=%async_computation.32 | async-start | bytes 2654208 | tf_op jit(solution)/shard_map/all_gather | solution.py:262
  1063.2 31.8 %copy-start.100 = (f32[1536]{0:T(1024)S(1)}, f32[1536]{0:T(1024)}, u32[]{:S(2)}) copy-start(f32[1536]{0:T(1024)} %copy-done.99) | copy-start | bytes 18436
  1065.4 76.0 %reduce-scatter.41.cloned.1.call-start = ((), (), s32[]{:S(2)}) async-start(), calls=%async_computation.33 | async-start | bytes 2654208 | tf_op jit(solution)/shard_map/reduce_scatter | solution.py:270
  1108.9 32.5 %copy-start.75 = (f32[768]{0:T(1024)S(1)}, f32[768]{0:T(1024)}, u32[]{:S(2)}) copy-start(f32[768]{0:T(1024)} %copy-done.74) | copy-start | bytes 9220
  1108.9 32.5 %copy-start.80 = (f32[288,2]{0,1:T(2,128)S(1)}, f32[288,2]{0,1:T(2,128)}, u32[]{:S(2)}) copy-start(f32[288,2]{0,1:T(2,128)} %copy-done.79) | copy-start | bytes 6916
  1108.9 32.5 %copy-start.86 = (f32[768]{0:T(1024)S(1)}, f32[768]{0:T(1024)}, u32[]{:S(2)}) copy-start(f32[768]{0:T(1024)} %copy-done.85) | copy-start | bytes 9220
  1113.0 31.0 %copy-start.94 = (f32[288,2]{0,1:T(2,128)S(1)}, f32[288,2]{0,1:T(2,128)}, u32[]{:S(2)}) copy-start(f32[288,2]{0,1:T(2,128)} %copy-done.93) | copy-start | bytes 6916
  1113.0 32.7 %copy-start.27 = (f32[288,2,768]{2,0,1:T(8,128)S(1)}, f32[288,2,768]{2,0,1:T(8,128)}, u32[]{:S(2)}) copy-start(f32[288,2,768]{2,0,1:T(8,128)} %copy-done.26) | copy-start | bytes 5308420
  1113.0 117.2 %all-gather.41.cloned.1.call-start = ((), (), s32[]{:S(2)}) async-start(), calls=%async_computation.34 | async-start | bytes 2654208 | tf_op jit(solution)/shard_map/all_gather | solution.py:281
  1149.4 270.3 %reduce-scatter.59.cloned.1.call-start = ((), (), s32[]{:S(2)}) async-start(), calls=%async_computation.43 | async-start | bytes 2506752 | tf_op jit(solution)/shard_map/reduce_scatter | solution.py:339
  1156.8 262.9 %reduce-scatter.57.cloned.1.call-start = ((), (), s32[]{:S(2)}) async-start(), calls=%async_computation.42 | async-start | bytes 2506752 | tf_op jit(solution)/shard_map/reduce_scatter | solution.py:339
  1163.5 258.1 %reduce-scatter.55.cloned.1.call-start = ((), (), s32[]{:S(2)}) async-start(), calls=%async_computation.41 | async-start | bytes 2506752 | tf_op jit(solution)/shard_map/reduce_scatter | solution.py:336
  1171.0 273.0 %reduce-scatter.53.cloned.1.call-start = ((), (), s32[]{:S(2)}) async-start(), calls=%async_computation.40 | async-start | bytes 2506752 | tf_op jit(solution)/shard_map/reduce_scatter | solution.py:336
  1230.1 305.4 %all-reduce.4.cloned.1.call-start = ((), (), s32[]{:S(2)}) async-start(), calls=%async_computation.54 | async-start | bytes 200704 | tf_op jit(solution)/shard_map/psum | solution.py:343
  1370.5 226.2 %reduce-scatter.51.cloned.1.call-start = ((), (), s32[]{:S(2)}) async-start(), calls=%async_computation.39 | async-start | bytes 626688 | tf_op jit(solution)/shard_map/reduce_scatter | solution.py:333
  1373.0 281.2 %reduce-scatter.49.cloned.1.call-start = ((), (), s32[]{:S(2)}) async-start(), calls=%async_computation.38 | async-start | bytes 626688 | tf_op jit(solution)/shard_map/reduce_scatter | solution.py:333
  1392.1 291.7 %reduce-scatter.43.cloned.1.call-start = ((), (), s32[]{:S(2)}) async-start(), calls=%async_computation.35 | async-start | bytes 2654208 | tf_op jit(solution)/shard_map/reduce_scatter | solution.py:310
  1401.1 346.6 %reduce-scatter.47.cloned.1.call-start = ((), (), s32[]{:S(2)}) async-start(), calls=%async_computation.37 | async-start | bytes 1880064 | tf_op jit(solution)/shard_map/reduce_scatter | solution.py:330
  1406.8 403.9 %reduce-scatter.45.cloned.1.call-start = ((), (), s32[]{:S(2)}) async-start(), calls=%async_computation.36 | async-start | bytes 1880064 | tf_op jit(solution)/shard_map/reduce_scatter | solution.py:330
  1413.2 270.6 %copy-start.5 = (bf16[288,2,768]{2,1,0:T(2,128)(2,1)S(1)}, bf16[288,2,768]{2,1,0:T(2,128)(2,1)}, u32[]{:S(2)}) copy-start(bf16[288,2,768]{2,1,0:T(2,128)(2,1)} %param.20) | copy-start | bytes 2654212
  1413.2 270.5 %copy-start.82 = (f32[288,2]{0,1:T(2,128)S(1)}, f32[288,2]{0,1:T(2,128)}, u32[]{:S(2)}) copy-start(f32[288,2]{0,1:T(2,128)} %copy-done.81) | copy-start | bytes 6916
  1413.2 270.5 %copy-start.88 = (f32[768]{0:T(1024)S(1)}, f32[768]{0:T(1024)}, u32[]{:S(2)}) copy-start(f32[768]{0:T(1024)} %copy-done.87) | copy-start | bytes 9220
  1413.2 453.5 %reduce-scatter.61.cloned.1.call-start = ((), (), s32[]{:S(2)}) async-start(), calls=%async_computation.50 | async-start | bytes 208896
  1416.1 269.5 %copy-start.103 = (f32[288,2]{0,1:T(2,128)S(1)}, f32[288,2]{0,1:T(2,128)}, u32[]{:S(2)}) copy-start(f32[288,2]{0,1:T(2,128)} %copy-done.102) | copy-start | bytes 6916
  1416.1 270.2 %copy-start.96 = (f32[288,2]{0,1:T(2,128)S(1)}, f32[288,2]{0,1:T(2,128)}, u32[]{:S(2)}) copy-start(f32[288,2]{0,1:T(2,128)} %copy-done.95) | copy-start | bytes 6916
  1655.7 160.6 %copy-start.23 = (f32[288,2,768]{2,0,1:T(8,128)S(1)}, f32[288,2,768]{2,0,1:T(8,128)}, u32[]{:S(2)}) copy-start(f32[288,2,768]{2,0,1:T(8,128)} %copy-done.22) | copy-start | bytes 5308420
  1683.8 132.5 %copy-start.33 = (bf16[288,2,768]{2,0,1:T(8,128)(2,1)S(1)}, bf16[288,2,768]{2,0,1:T(8,128)(2,1)}, u32[]{:S(2)}) copy-start(bf16[288,2,768]{2,0,1:T(8,128)(2,1)} %reduce-scatter.43.cloned.1.call-done) | copy-start | bytes 2654212
  1701.2 221.6 %reduce-scatter.63.cloned.1.call-start = ((), (), s32[]{:S(2)}) async-start(), calls=%async_computation.51 | async-start | bytes 208896
  1814.0 164.9 %reduce-scatter.65.cloned.1.call-start = ((), (), s32[]{:S(2)}) async-start(), calls=%async_computation.52 | async-start | bytes 208896
  1816.2 218.9 %reduce-scatter.67.cloned.1.call-start = ((), (), s32[]{:S(2)}) async-start(), calls=%async_computation.53 | async-start | bytes 208896
  (139 other events, 773.4 us)
Sparse Core Ops, SparseCore 0:
  73.0 27.8 all-gather.26
  103.7 40.5 all-gather.42
  236.2 27.1 reduce-scatter.28
  266.3 42.2 all-gather.44
  310.6 28.1 all-gather.28
  341.8 42.2 all-gather.46
  391.1 27.0 reduce-scatter.30
  420.5 40.4 all-gather.48
  463.1 28.3 all-gather.30
  598.3 25.6 reduce-scatter.32
  627.1 42.2 all-gather.50
  671.4 28.1 all-gather.32
  701.3 29.4 all-gather.34
  733.7 42.2 all-gather.52
  794.2 26.9 reduce-scatter.36
  823.3 28.2 reduce-scatter.34
  858.0 29.4 all-gather.36
  1029.7 28.2 reduce-scatter.38
  1065.6 29.4 all-gather.38
  1113.1 28.2 reduce-scatter.40
  1149.5 29.4 all-gather.40
  1183.3 62.9 reduce-scatter.58
  1250.0 61.9 reduce-scatter.56
  1316.1 62.0 reduce-scatter.54
  1381.9 61.9 reduce-scatter.52
  1449.9 85.5 all-reduce.3
  1539.3 57.3 reduce-scatter.50
  1600.3 53.8 reduce-scatter.48
  1656.6 27.1 reduce-scatter.42
  1687.4 60.2 reduce-scatter.46
  1751.5 59.1 reduce-scatter.44
  1814.2 52.5 reduce-scatter.60
  1870.1 52.6 reduce-scatter.62
  1926.3 52.5 reduce-scatter.64
  1982.4 52.5 reduce-scatter.66
where the time goes:
time: 2050 us; the launch traced here: 2040 us
  waiting for transfers between devices  1010 us (49%)
  local copies, waits for them, and re-layouts  464 us (23%)
  matrix products  249 us (12%)
  other arithmetic  160 us (8%)
  blocking collectives  135 us (7%)
    unnamed x39, waiting for transfers between devices  210 us
    reduce_scatter x2, waiting for transfers between devices, shards(): lax.psum_scatter(proj_grad.astype(jnp.bfloat16), 'dp', scatter_dimension=...  115 us
    reduce_scatter x2, waiting for transfers between devices, shards(): lax.psum_scatter(qkv_grad.astype(jnp.bfloat16), 'dp', scatter_dimension=0...  109 us
    psum x1, waiting for transfers between devices, shards(): small_grads = lax.psum((qv_grad, fc1_bias_grad, table_grad), 'dp')  89.7 us
    all_gather x2, waiting for transfers between devices, shards(): lax.all_gather(w_fc1[layer_index], 'dp', axis=0, tiled=True)  77.1 us
    unnamed x274, local copies, waits for them, and re-layouts  71.7 us
    reshape x4, local copies, waits for them, and re-layouts, table_back(): shaped = score_sum.reshape(score_sum.shape[0], WIN, WIN, WIN, WIN)  62.9 us
    all_gather x2, waiting for transfers between devices, shards(): lax.all_gather(w_fc2[layer_index], 'dp', axis=1, tiled=True)  62.8 us
  transfers between devices with their start and end apart: 35, of which 27 were waited for; matrix products, arithmetic and copies ran while one was open for 21% of the time, Pallas kernels for 0%

commit v1 on v0

--- a/solution.py
+++ b/solution.py
@@ -1,6 +1,10 @@
+import functools
+import numpy as np
 import jax
 import jax.numpy as jnp
 from jax import lax
+from jax.experimental import pallas as pl
+from jax.experimental.pallas import tpu as pltpu
 from jax.sharding import PartitionSpec as P
 
 WIN = 12
@@ -9,10 +13,829 @@
 SIDE = 24
 SHIFT = 6
 RELS = 529
-
-
 EPSILON = 1e-05
 MASK_FILL = -100.0
+
+D = 768
+HEADS = 24
+FF = 3072
+TOK = 576
+WT = 144
+UC = 384
+NU = 12
+HG = 4
+NG = HEADS // HG
+SCALE = HDIM ** -0.5
+BF = jnp.bfloat16
+F32 = jnp.float32
+
+
+def nn(a, b):
+    return lax.dot_general(a, b, (((1,), (0,)), ((), ())), preferred_element_type=F32)
+
+
+def nt(a, b):
+    return lax.dot_general(a, b, (((1,), (1,)), ((), ())), preferred_element_type=F32)
+
+
+def norm_parts(x):
+    mean = jnp.mean(x, axis=-1, keepdims=True)
+    c = x - mean
+    var = jnp.mean(c * c, axis=-1, keepdims=True)
+    rstd = lax.rsqrt(var + EPSILON)
+    return c * rstd, rstd
+
+
+def gelu_parts(u):
+    phi_big = 0.5 * (1.0 + lax.erf(u * (0.5 ** 0.5)))
+    phi = jnp.exp(-0.5 * u * u) * (1.0 / (2.0 * np.pi) ** 0.5)
+    return u * phi_big, phi_big + u * phi
+
+
+def window_order():
+    out = []
+    for shift in (0, SHIFT):
+        p = np.arange(SIDE)
+        src = (p + shift) % SIDE
+        grid = src[:, None] * SIDE + src[None, :]
+        grid = grid.reshape(2, WIN, 2, WIN).transpose(0, 2, 1, 3).reshape(TOK)
+        out.append(grid)
+    return np.stack(out)
+
+
+def perm_matrices():
+    order = window_order()
+    return (order[:, :, None] == np.arange(TOK)[None, None, :]).astype(np.float32)
+
+
+def shift_mask():
+    places = np.arange(SIDE)
+    band_of = (places >= SIDE - WIN).astype(np.int32) + (places >= SIDE - SHIFT).astype(np.int32)
+    region = band_of[:, None] * 3 + band_of[None, :]
+    region = region.reshape(2, WIN, 2, WIN).transpose(0, 2, 1, 3).reshape(4, WT)
+    same = region[:, :, None] == region[:, None, :]
+    masked = np.where(same, 0.0, MASK_FILL).astype(np.float32)
+    return np.stack([np.zeros_like(masked), masked])
+
+
+def rows_loop(n, body):
+    def step(i, c):
+        body(i)
+        return c
+    lax.fori_loop(0, n, step, 0)
+
+
+def w2d(wbuf, slot, t):
+    return wbuf[slot, t].reshape(D, UC)
+
+
+class Place:
+    def __init__(self):
+        d, self.t = lax.axis_index("dp"), lax.axis_index("tensor")
+        self.z = lax.div(d, 4)
+        self.y = lax.rem(lax.div(d, 2), 2)
+        self.c = lax.rem(d, 2)
+        t, y, even = self.t, self.y, self.c == 0
+        self.x_side, self.y_side = (1 - t, y), (t, 1 - y)
+        self.first = tuple(jnp.where(even, a, b) for a, b in zip(self.x_side, self.y_side))
+        self.second = tuple(jnp.where(even, b, a) for a, b in zip(self.x_side, self.y_side))
+        self.diagonal = (1 - t, 1 - y)
+
+    def device(self, z, ty, c):
+        return {"dp": (z * 2 + ty[1]) * 2 + c, "tensor": ty[0]}
+
+    def side(self, ty):
+        return self.device(self.z, ty, self.c)
+
+    def along(self, k):
+        return lax.rem(self.z + k, 4)
+
+    def above(self, k):
+        return self.device(self.along(k), (self.t, self.y), self.c)
+
+    def sibling(self):
+        return self.device(self.z, (self.t, self.y), 1 - self.c)
+
+    def barrier(self):
+        sem = pltpu.get_barrier_semaphore()
+        peers = [self.above(k) for k in (1, 2, 3)] + [self.side(self.x_side), self.side(self.y_side), self.sibling()]
+        for peer in peers:
+            pl.semaphore_signal(sem, inc=1, device_id=peer, device_id_type=MESH)
+        pl.semaphore_wait(sem, len(peers))
+
+
+MESH = pl.DeviceIdType.MESH
+GATHER_LAGS = (1, 2, 3, 4)
+GATHER_SEMS = 8
+TICK_EVERY = 4
+
+
+class Gather:
+    def __init__(self, at, shard, whole, send, recv, local, units):
+        self.at, self.shard, self.whole, self.units = at, shard, whole, units
+        self.send, self.recv, self.local = send, recv, local
+
+    def copy(self, g, n, src, dst, device):
+        slot = lax.rem(g, GATHER_SEMS) if self.units > 1 else 0
+        return pltpu.make_async_remote_copy(
+            src_ref=src, dst_ref=dst, send_sem=self.send.at[slot, n], recv_sem=self.recv.at[slot, n],
+            device_id=device, device_id_type=MESH)
+
+    def mine(self, g):
+        p = self.at
+        return pltpu.make_async_copy(self.shard.at[g], self.whole.at[g, p.t, p.z, p.y, p.c],
+                                     self.local.at[lax.rem(g, GATHER_SEMS) if self.units > 1 else 0])
+
+    def up(self, g, k):
+        p = self.at
+        return self.copy(g, k - 1, self.shard.at[g], self.whole.at[g, p.t, p.z, p.y, p.c], p.above(k))
+
+    def group(self, g, n, ty, to):
+        ref = self.whole.at[g, ty[0], :, ty[1], self.at.c]
+        return self.copy(g, n, ref, ref, self.at.side(to))
+
+    def first(self, g):
+        return self.group(g, 3, (self.at.t, self.at.y), self.at.first)
+
+    def second(self, g):
+        return self.group(g, 4, (self.at.t, self.at.y), self.at.second)
+
+    def onward(self, g):
+        return self.group(g, 5, self.at.first, self.at.second)
+
+    def core(self, g):
+        ref = self.whole.at[g, :, :, :, self.at.c]
+        return self.copy(g, 6, ref, ref, self.at.sibling())
+
+    def stage(self, n, g):
+        if n == 0:
+            self.mine(g).start()
+            for k in (1, 2, 3):
+                self.up(g, k).start()
+        elif n == 1:
+            self.mine(g).wait()
+            for k in (1, 2, 3):
+                self.up(g, k).wait_recv()
+            self.first(g).start()
+            self.second(g).start()
+        elif n == 2:
+            self.first(g).wait_recv()
+            self.onward(g).start()
+        elif n == 3:
+            self.second(g).wait_recv()
+            self.onward(g).wait_recv()
+            self.core(g).start()
+        else:
+            self.core(g).wait()
+            for k in (1, 2, 3):
+                self.up(g, k).wait_send()
+            self.first(g).wait_send()
+            self.second(g).wait_send()
+            self.onward(g).wait_send()
+
+    def tick(self, n):
+        for st in (4, 3, 2, 1, 0):
+            g = n - (GATHER_LAGS[st - 1] if st else 0)
+            if isinstance(g, int):
+                if 0 <= g < self.units:
+                    self.stage(st, g)
+            else:
+                @pl.when((g >= 0) & (g < self.units))
+                def _(st=st, g=g):
+                    self.stage(st, g)
+
+
+def fold_places():
+    lane = np.arange(UC)
+    j, xb = lane // WIN, lane % WIN
+    return np.where(j < 2 * WIN - 1, (2 * WIN - 2 - j) * (2 * WIN - 1) - xb + WIN - 1, -4 * PAY).astype(np.int32)[None]
+
+
+def fold_matrix(places, xa):
+    rows = lax.broadcasted_iota(jnp.int32, (PAY, UC), 0)
+    return jnp.where(rows == places + xa, 1.0, 0.0).astype(BF)
+
+
+def split3(x):
+    hi = x.astype(BF)
+    rest = x - hi.astype(F32)
+    mid = rest.astype(BF)
+    return hi, mid, (rest - mid.astype(F32)).astype(BF)
+
+
+def half_rows(t):
+    return pl.ds(pl.multiple_of(t * HALF, HALF), HALF)
+
+
+def forward_kernel(tok, cot, valid, vshard, pay, places, mask, perm, permt, shard,
+                   out, vec, cot_h, w_hbm, x0_h, x1_h, n1_h, qkv_h, pw_h, o_h, n2_h, gg_h,
+                   wbuf, x0, x1, n1, qkv, ow, n2, acc, pst, gst, ubuf,
+                   xin, vall, pays, ext, bias,
+                   wsem, ssem, psem, gsem, gsend, grecv, glocal, vsend, vrecv, vlocal, xsend, xrecv, xlocal):
+    at = Place()
+    ag = Gather(at, shard, w_hbm, gsend, grecv, glocal, LAYERS * NU)
+    vg = Gather(at, vshard, vall, vsend, vrecv, vlocal, 1)
+    at.barrier()
+    lag = GATHER_LAGS[-1]
+    t = at.t
+    mine, theirs = half_rows(t), half_rows(1 - t)
+    swaps, keeps = [], []
+    for n, (src, here, src_keep) in enumerate((
+            (tok.at[1 - t], xin.at[mine], tok.at[t]),
+            (pay, pays.at[t], pay),
+            (cot.at[1 - t], cot_h.at[mine], cot.at[t]))):
+        swaps.append(pltpu.make_async_remote_copy(
+            src_ref=src, dst_ref=here, send_sem=xsend.at[n], recv_sem=xrecv.at[n],
+            device_id=at.side(at.x_side), device_id_type=MESH))
+        keeps.append(pltpu.make_async_copy(src_keep, here, xlocal.at[n]))
+    for n in range(2):
+        swaps[n].start()
+        keeps[n].start()
+    for n in range(lag + 1):
+        vg.tick(n)
+        ag.tick(n)
+        if n == 0:
+            swaps[1].wait()
+            keeps[1].wait()
+            table = jnp.concatenate([pays[0, 16:40], pays[1, 16:40]], axis=0)
+            parts = jnp.concatenate(split3(table), axis=0)
+            for xa in range(WIN):
+                y = nn(parts, fold_matrix(places[...], xa))
+                ext[:, xa, :] = y[:48] + y[48:96] + y[96:]
+    for n in range(2, 3):
+        swaps[n].start()
+        keeps[n].start()
+
+    def spread(i, c):
+        half, l, h = lax.div(i, 24), lax.rem(lax.div(i, 12), 2), lax.rem(i, 12)
+        x = ext[i]
+        for ya in range(WIN):
+            off = (WIN - 1 - ya) * WIN
+            bias[l, half * 12 + h, ya * WIN:(ya + 1) * WIN, :] = x[:, off:off + WT]
+        return c
+    lax.fori_loop(0, 48, spread, 0)
+    vec[...] = vall[0, 0].reshape(D, 128).astype(F32).T[:16]
+    swaps[0].wait()
+    keeps[0].wait()
+
+    def vrow(l, i):
+        return vec[pl.ds(l * 6 + i, 1)]
+
+    def fetch(g, u):
+        return pltpu.make_async_copy(w_hbm.at[g], wbuf.at[u % 2], wsem.at[u % 2])
+
+    def tick_base(l, u):
+        inside = 4 * NG // TICK_EVERY
+        return lag + 1 + l * (NU + inside) + u + (inside if u > 3 else 0)
+
+    def step_unit(l, u):
+        g = l * NU + u
+        fetch(g, u).wait()
+        ag.tick(tick_base(l, u) + (4 * NG // TICK_EVERY if u == 3 else 0))
+
+        @pl.when(g + 1 < LAYERS * NU)
+        def _():
+            fetch(g + 1, u + 1).start()
+
+    fetch(0, 0).start()
+    x0[0] = xin[...].astype(F32)
+    lanes = lax.shift_right_logical(lax.broadcasted_iota(jnp.int32, (WT, HG * HDIM), 1), 5)
+
+    def layer(l, carry):
+        x0_l, x1_l, n1_l, n2_l, ow_l = x0.at[l], x1.at[l], n1.at[l], n2.at[l], ow.at[l]
+
+        def ln1(i):
+            r = pl.ds(i * WT, WT)
+            xh, _ = norm_parts(x0_l[r])
+            ow_l[r] = (xh * vrow(l, 0) + vrow(l, 2)).astype(BF)
+        rows_loop(4, ln1)
+        n1_l[...] = nn(perm[l], ow_l[...]).astype(BF)
+        for j in range(3):
+            step_unit(l, j)
+            for t in range(2):
+                cols = slice(t * UC, (t + 1) * UC)
+                y = nn(n1_l[...], w2d(wbuf, j % 2, t))
+                if j == 0:
+                    y = y + pays[t, pl.ds(l * 2, 1), :UC]
+                if j == 2:
+                    y = y + pays[t, pl.ds(l * 2 + 1, 1), :UC]
+                qkv[l, j, :, cols] = y.astype(BF)
+
+        def attend(it, c):
+            w, hg = lax.div(it, NG), lax.rem(it, NG)
+            r = pl.ds(pl.multiple_of(w * WT, WT), WT)
+            cl = pl.ds(pl.multiple_of(hg * 128, 128), 128)
+            slot = lax.rem(it, 2)
+            q, k, v = qkv[l, 0, r, cl], qkv[l, 1, r, cl], qkv[l, 2, r, cl]
+            put = pltpu.make_async_copy(pst.at[slot], pw_h.at[l, w, pl.ds(hg * HG, HG)], psem.at[slot])
+
+            @pl.when((it >= 2) | (l > 0))
+            def _():
+                put.wait()
+            o = jnp.zeros((WT, 128), F32)
+            for h in range(HG):
+                qm = jnp.where(lanes == h, q, jnp.zeros_like(q))
+                s = nt(qm, k) * SCALE + bias[l, hg * HG + h] + mask[l, w]
+                e = jnp.exp(s - jnp.max(s, axis=-1, keepdims=True))
+                p = (e * (1.0 / jnp.sum(e, axis=-1, keepdims=True))).astype(BF)
+                pst[slot, h] = p
+                o = jnp.where(lanes == h, nn(p, v), o)
+            ow_l[r, cl] = o.astype(BF)
+            put.start()
+
+            @pl.when(lax.rem(it, TICK_EVERY) == TICK_EVERY - 1)
+            def _():
+                ag.tick(tick_base(l, 3) + lax.div(it, TICK_EVERY))
+            return c
+        lax.fori_loop(0, 4 * NG, attend, 0)
+        n2_l[...] = nn(permt[l], ow_l[...]).astype(BF)
+        step_unit(l, 3)
+        for t in range(2):
+            y = nt(n2_l[:, t * UC:(t + 1) * UC], w2d(wbuf, 1, t))
+            if t == 0:
+                acc[...] = y
+            else:
+                acc[...] += y
+
+        def ln2(i):
+            r = pl.ds(i * WT, WT)
+            x = x0_l[r] + acc[r] + vrow(l, 3)
+            x1_l[r] = x
+            xh, _ = norm_parts(x)
+            n2_l[r] = (xh * vrow(l, 1) + vrow(l, 4)).astype(BF)
+            acc[r] = x + vrow(l, 5)
+        rows_loop(4, ln2)
+        for i in range(4):
+            step_unit(l, 4 + 2 * i)
+            for t in range(2):
+                put = pltpu.make_async_copy(gst.at[t], gg_h.at[l, i, t], gsem.at[t])
+                if i > 0:
+                    put.wait()
+                else:
+                    @pl.when(l > 0)
+                    def _():
+                        put.wait()
+                ubuf[...] = nn(n2_l[...], w2d(wbuf, 0, t)) + pays[t, pl.ds(4 + l * 4 + i, 1), :UC]
+
+                def act(n):
+                    r = pl.ds(n * 96, 96)
+                    g, gp = gelu_parts(ubuf[r])
+                    gst[t, 0, r] = g.astype(BF)
+                    gst[t, 1, r] = gp.astype(BF)
+                rows_loop(6, act)
+                put.start()
+            step_unit(l, 5 + 2 * i)
+            for t in range(2):
+                acc[...] += nt(gst[t, 0], w2d(wbuf, 1, t))
+
+        for ref, dst in ((x0, x0_h), (x1, x1_h), (n1, n1_h), (qkv, qkv_h), (ow, o_h), (n2, n2_h)):
+            pltpu.make_async_copy(ref.at[l], dst.at[l], ssem.at[l]).start()
+
+        @pl.when(l == 0)
+        def _():
+            x0[1] = acc[...]
+
+        @pl.when(l == 1)
+        def _():
+            out[...] = (acc[...] * valid[0].astype(F32)).astype(BF)
+        return carry
+    lax.fori_loop(0, LAYERS, layer, 0)
+    for l in range(LAYERS):
+        for ref, dst in ((x0, x0_h), (x1, x1_h), (n1, n1_h), (qkv, qkv_h), (ow, o_h), (n2, n2_h)):
+            pltpu.make_async_copy(ref.at[l], dst.at[l], ssem.at[l]).wait()
+    for s in range(2):
+        pltpu.make_async_copy(pst.at[s], pw_h.at[0, 0, pl.ds(0, HG)], psem.at[s]).wait()
+        pltpu.make_async_copy(gst.at[s], gg_h.at[0, 0, s], gsem.at[s]).wait()
+    swaps[2].wait()
+    keeps[2].wait()
+
+
+def sds(shape, dtype):
+    return jax.ShapeDtypeStruct(shape, dtype)
+
+
+VM = pl.BlockSpec(memory_space=pltpu.VMEM)
+AN = pl.BlockSpec(memory_space=pl.ANY)
+SM = pl.BlockSpec(memory_space=pltpu.SMEM)
+
+SAVED = [
+    sds((LAYERS, TOK, D), F32), sds((LAYERS, TOK, D), F32), sds((LAYERS, TOK, D), BF),
+    sds((LAYERS, 3, TOK, D), BF), sds((LAYERS, 4, HEADS, WT, WT), BF),
+    sds((LAYERS, TOK, D), BF), sds((LAYERS, TOK, D), BF), sds((LAYERS, 4, 2, 2, TOK, UC), BF),
+]
+
+
+def forward_call(tok, cot, valid, vshard, pay, shard):
+    perm = perm_matrices()
+    permt = jnp.asarray(perm.transpose(0, 2, 1), BF)
+    return pl.pallas_call(
+        forward_kernel,
+        out_shape=[sds((TOK, D), BF), sds((16, D), F32), sds((TOK, D), BF),
+                   sds((LAYERS * NU, 2, 4, 2, 2, 48, UC), BF)] + SAVED,
+        in_specs=[AN, AN, SM, AN, AN, VM, VM, VM, VM, AN],
+        out_specs=[VM, VM] + [AN] * 10,
+        scratch_shapes=[
+            pltpu.VMEM((2, 2, 4, 2, 2, 48, UC), BF),
+            pltpu.VMEM((2, TOK, D), F32), pltpu.VMEM((2, TOK, D), F32),
+            pltpu.VMEM((2, TOK, D), BF), pltpu.VMEM((2, 3, TOK, D), BF),
+            pltpu.VMEM((2, TOK, D), BF), pltpu.VMEM((2, TOK, D), BF),
+            pltpu.VMEM((TOK, D), F32), pltpu.VMEM((2, HG, WT, WT), BF),
+            pltpu.VMEM((2, 2, TOK, UC), BF), pltpu.VMEM((TOK, UC), F32),
+            pltpu.VMEM((TOK, D), BF), pltpu.VMEM((1, 2, 4, 2, 2, 48, 128), BF),
+            pltpu.VMEM((2, 40, PAY), F32), pltpu.VMEM((48, WIN, UC), F32),
+            pltpu.VMEM((LAYERS, HEADS, WT, WT), F32),
+            pltpu.SemaphoreType.DMA((2,)), pltpu.SemaphoreType.DMA((2,)),
+            pltpu.SemaphoreType.DMA((2,)), pltpu.SemaphoreType.DMA((2,)),
+            pltpu.SemaphoreType.DMA((GATHER_SEMS, 7)), pltpu.SemaphoreType.DMA((GATHER_SEMS, 7)),
+            pltpu.SemaphoreType.DMA((GATHER_SEMS,)),
+            pltpu.SemaphoreType.DMA((1, 7)), pltpu.SemaphoreType.DMA((1, 7)), pltpu.SemaphoreType.DMA((1,)),
+            pltpu.SemaphoreType.DMA((3,)), pltpu.SemaphoreType.DMA((3,)), pltpu.SemaphoreType.DMA((3,)),
+        ],
+        compiler_params=pltpu.CompilerParams(vmem_limit_bytes=60 * 2**20, collective_id=0, has_side_effects=True),
+        name="forward",
+    )(tok, cot, valid, vshard, pay, fold_places(), shift_mask(), jnp.asarray(perm, BF), permt, shard)
+
+
+BACK_ORDER = (5, 4, 7, 6, 9, 8, 11, 10, 3, 0, 1, 2)
+
+
+def norm_back(x, dn, gain):
+    xh, rstd = norm_parts(x)
+    dx = dn * gain
+    grad = rstd * (dx - jnp.mean(dx, axis=-1, keepdims=True)
+                   - xh * jnp.mean(dx * xh, axis=-1, keepdims=True))
+    return grad, jnp.sum(dn * xh, axis=0, keepdims=True), jnp.sum(dn, axis=0, keepdims=True)
+
+
+REDUCE_SLOTS = 8
+PAY = 640
+HALF = TOK // 2
+VIRT = 16
+GAP = (9, 13)
+REDUCE_LAGS = (1, 2, 3, 4)
+
+
+class Reduce:
+    def __init__(self, at, own, core_in, first_in, second_in, z_in, total, send, recv):
+        self.at, self.own, self.total = at, own, total
+        self.core_in, self.first_in, self.second_in, self.z_in = core_in, first_in, second_in, z_in
+        self.send, self.recv = send, recv
+
+    def copy(self, v, n, src, dst, device):
+        slot = lax.rem(v, REDUCE_SLOTS)
+        return pltpu.make_async_remote_copy(
+            src_ref=src, dst_ref=dst, send_sem=self.send.at[slot, n], recv_sem=self.recv.at[slot, n],
+            device_id=device, device_id_type=MESH)
+
+    def core(self, v):
+        slot = lax.rem(v, REDUCE_SLOTS)
+        return self.copy(v, 0, self.own.at[slot, :, :, :, 1 - self.at.c], self.core_in.at[slot], self.at.sibling())
+
+    def group(self, v, ty):
+        return self.own.at[lax.rem(v, REDUCE_SLOTS), ty[0], :, ty[1], self.at.c]
+
+    def first(self, v, n):
+        p = self.at
+        ty = p.diagonal if n == 0 else p.second
+        return self.copy(v, 1 + n, self.group(v, ty), self.first_in.at[lax.rem(v, REDUCE_SLOTS), n], p.side(p.second))
+
+    def second(self, v):
+        p = self.at
+        return self.copy(v, 3, self.group(v, p.first), self.second_in.at[lax.rem(v, REDUCE_SLOTS)], p.side(p.first))
+
+    def up(self, v, k):
+        p, slot = self.at, lax.rem(v, REDUCE_SLOTS)
+        return self.copy(v, 3 + k, self.own.at[slot, p.t, p.along(k), p.y, p.c], self.z_in.at[slot, k - 1], p.above(k))
+
+    def add(self, ref, other):
+        def one(z):
+            ref[z] = ref[z] + other[z]
+        rows_loop(4, one)
+
+    def stage(self, n, v):
+        p, slot = self.at, lax.rem(v, REDUCE_SLOTS)
+        if n == 0:
+            self.core(v).start()
+        elif n == 1:
+            self.core(v).wait_recv()
+
+            def one(i):
+                t, z = lax.div(i, 4), lax.rem(i, 4)
+                self.own[slot, t, z, :, p.c] = self.own[slot, t, z, :, p.c] + self.core_in[slot, t, z]
+            rows_loop(8, one)
+            self.first(v, 0).start()
+            self.first(v, 1).start()
+        elif n == 2:
+            self.first(v, 0).wait_recv()
+            self.add(self.group(v, p.first), self.first_in.at[slot, 0])
+            self.second(v).start()
+            self.first(v, 1).wait_recv()
+            self.add(self.group(v, (p.t, p.y)), self.first_in.at[slot, 1])
+        elif n == 3:
+            self.second(v).wait_recv()
+            self.add(self.group(v, (p.t, p.y)), self.second_in.at[slot])
+            for k in (1, 2, 3):
+                self.up(v, k).start()
+        else:
+            total = self.own[slot, p.t, p.z, p.y, p.c].astype(F32)
+            for k in (1, 2, 3):
+                self.up(v, k).wait_recv()
+                total = total + self.z_in[slot, k - 1].astype(F32)
+            self.total[v] = total
+            self.core(v).wait_send()
+            for n in range(2):
+                self.first(v, n).wait_send()
+            self.second(v).wait_send()
+            for k in (1, 2, 3):
+                self.up(v, k).wait_send()
+
+    def tick(self, n):
+        for st in (4, 3, 2, 1, 0):
+            v = n - (REDUCE_LAGS[st - 1] if st else 0)
+            place = lax.rem(v, VIRT)
+
+            @pl.when((v >= 0) & (v < LAYERS * VIRT) & ((place < GAP[0]) | (place >= GAP[1])))
+            def _(st=st, v=v):
+                self.stage(st, v)
+
+
+def backward_kernel(cot, valid, vec, places, perm, permt, block, w_hbm, x0_h, x1_h, n1_h, qkv_h, pw_h, o_h, n2_h, gg_h,
+                    gt, block2, total, small,
+                    e, sums, folded, dsum, sm_core, sm_x, sm_y, sm_z, gin,
+                    wbuf, xb, n1, n2, qkv, ow, do, dqkv, acc, em, emt, n2t, pst, gst, ubuf, dub, gbuf,
+                    core_in, first_in, second_in, z_in,
+                    wsem, lsem, psem, gsem, rsend, rrecv, xsend, xrecv, xlocal, ssend, srecv):
+    at = Place()
+    t_here = at.t
+    mine, theirs = half_rows(t_here), half_rows(1 - t_here)
+    rs = Reduce(at, gbuf, core_in, first_in, second_in, z_in, total, rsend, rrecv)
+
+    def fetch(g, pos):
+        return pltpu.make_async_copy(w_hbm.at[g], wbuf.at[pos % 2], wsem.at[pos % 2])
+
+    def step_unit(l, pos):
+        fetch(0, pos).wait()
+        if pos + 1 < NU:
+            fetch(l * NU + BACK_ORDER[pos + 1], pos + 1).start()
+        else:
+            @pl.when(l > 0)
+            def _():
+                fetch((l - 1) * NU + BACK_ORDER[0], 0).start()
+
+    def place_of(pos):
+        return pos if pos < GAP[0] else pos + GAP[1] - GAP[0]
+
+    def emit(l, pos, t, value):
+        v = place_of(pos)
+        gbuf[v % REDUCE_SLOTS, t] = value.astype(BF).reshape(4, 2, 2, 48, UC)
+        if t == 1:
+            rs.tick((LAYERS - 1 - l) * VIRT + v)
+
+    fetch((LAYERS - 1) * NU + BACK_ORDER[0], 0).start()
+    at.barrier()
+    block_swap = pltpu.make_async_remote_copy(
+        src_ref=block.at[theirs], dst_ref=block2.at[t_here], send_sem=xsend.at[0], recv_sem=xrecv.at[0],
+        device_id=at.side(at.x_side), device_id_type=MESH)
+    block_keep = pltpu.make_async_copy(block.at[mine], block2.at[t_here], xlocal.at[0])
+    block_swap.start()
+    block_keep.start()
+    total[...] = jnp.zeros_like(total)
+    e[...] = cot[...].astype(F32) * valid[0].astype(F32)
+    sums[...] = jnp.zeros_like(sums)
+    lanes = lax.shift_right_logical(lax.broadcasted_iota(jnp.int32, (WT, HG * HDIM), 1), 5)
+
+    def layer(step, carry):
+        l = LAYERS - 1 - step
+        loads = [pltpu.make_async_copy(src.at[l], dst, lsem.at[n]) for n, (src, dst) in enumerate((
+            (n2_h, n2), (x1_h, xb.at[1]), (o_h, ow), (qkv_h, qkv), (n1_h, n1), (x0_h, xb.at[0])))]
+        for cp in loads:
+            cp.start()
+
+        def load_gg(k):
+            return pltpu.make_async_copy(gg_h.at[l, k // 2, k % 2], gst.at[k % 2], gsem.at[k % 2])
+        load_gg(0).start()
+        load_gg(1).start()
+
+        def ends(i):
+            r = pl.ds(i * WT, WT)
+            x = e[r]
+            em[r] = x.astype(BF)
+            sums[l, 2, 5:6] += jnp.sum(x, axis=0, keepdims=True)
+        rows_loop(4, ends)
+        emt[...] = em[...].T
+        loads[0].wait()
+        n2t[...] = n2[...].T
+        for i in range(4):
+            step_unit(l, 2 * i)
+            for t in range(2):
+                load_gg(2 * i + t).wait()
+                ubuf[...] = nn(em[...], w2d(wbuf, 0, t))
+
+                def act(n):
+                    r = pl.ds(n * 96, 96)
+                    du = (ubuf[r] * gst[t, 1, r].astype(F32)).astype(BF)
+                    dub[t, r] = du
+                    sums[l, t, 14 + i // 2:15 + i // 2, (i % 2) * UC:(i % 2 + 1) * UC] += jnp.sum(du.astype(F32), axis=0, keepdims=True)
+                rows_loop(6, act)
+                emit(l, 2 * i, t, nn(emt[...], gst[t, 0]))
+                if i < 3:
+                    load_gg(2 * i + t + 2).start()
+            step_unit(l, 2 * i + 1)
+            for t in range(2):
+                y = nt(dub[t], w2d(wbuf, 1, t))
+                if i == 0 and t == 0:
+                    acc[...] = y
+                else:
+                    acc[...] += y
+                emit(l, 2 * i + 1, t, nn(n2t[...], dub[t]))
+        loads[1].wait()
+
+        def ln2(i):
+            r = pl.ds(i * WT, WT)
+            grad, gsum, bsum = norm_back(xb[1, r], acc[r], vec[pl.ds(l * 6 + 1, 1)])
+            x = e[r] + grad
+            e[r] = x
+            em[r] = x.astype(BF)
+            sums[l, 2, 1:2] += gsum
+            sums[l, 2, 4:5] += bsum
+            sums[l, 2, 3:4] += jnp.sum(x, axis=0, keepdims=True)
+        rows_loop(4, ln2)
+        n2[...] = nn(perm[l], em[...]).astype(BF)
+        emt[...] = n2[...].T
+        step_unit(l, 8)
+        loads[2].wait()
+        for t in range(2):
+            cols = slice(t * UC, (t + 1) * UC)
+            do[:, cols] = nn(n2[...], w2d(wbuf, 0, t)).astype(BF)
+            emit(l, 8, t, nn(emt[...], ow[:, cols]))
+        loads[3].wait()
+
+        def load_pw(it):
+            w, hg = lax.div(it, NG), lax.rem(it, NG)
+            return pltpu.make_async_copy(pw_h.at[l, w, pl.ds(hg * HG, HG)], pst.at[lax.rem(it, 2)], psem.at[lax.rem(it, 2)])
+        load_pw(0).start()
+        dsum[...] = jnp.zeros_like(dsum)
+
+        def attend(it, c):
+            w, hg = lax.div(it, NG), lax.rem(it, NG)
+            r = pl.ds(pl.multiple_of(w * WT, WT), WT)
+            cl = pl.ds(pl.multiple_of(hg * 128, 128), 128)
+            slot = lax.rem(it, 2)
+
+            @pl.when(it + 1 < 4 * NG)
+            def _():
+                load_pw(it + 1).start()
+            q, k, v, d = qkv[0, r, cl], qkv[1, r, cl], qkv[2, r, cl], do[r, cl]
+            qt, dt = q.T, d.T
+            load_pw(it).wait()
+            dq = jnp.zeros((WT, 128), F32)
+            dkt, dvt = [], []
+            for h in range(HG):
+                pw = pst[slot, h]
+                p = pw.astype(F32)
+                dp = nt(jnp.where(lanes == h, d, jnp.zeros_like(d)), v)
+                mean = jnp.sum(p * dp, axis=-1, keepdims=True) / jnp.sum(p, axis=-1, keepdims=True)
+                ds = (p * (dp - mean)).astype(BF)
+                dsum[hg * HG + h, :, :WT] += ds.astype(F32)
+                hr = slice(h * HDIM, (h + 1) * HDIM)
+                dvt.append(nn(dt[hr], pw))
+                dkt.append(nn(qt[hr], ds))
+                dq = jnp.where(lanes == h, nn(ds, k), dq)
+            dqkv[0, r, cl] = (dq * SCALE).astype(BF)
+            dqkv[1, r, cl] = (jnp.concatenate(dkt, axis=0) * SCALE).T.astype(BF)
+            dqkv[2, r, cl] = jnp.concatenate(dvt, axis=0).T.astype(BF)
+
+            @pl.when(lax.rem(it, 6) == 5)
+            def _():
+                rs.tick(step * VIRT + GAP[0] + lax.div(it, 6))
+            return c
+        lax.fori_loop(0, 4 * NG, attend, 0)
+
+        def fold(h, c):
+            x = jnp.zeros((WIN, UC), F32)
+            for ya in range(WIN):
+                x = x + pltpu.roll(dsum[h, ya * WIN:(ya + 1) * WIN, :], (WIN - 1 - ya) * WIN, 1)
+            folded[h] = x
+            return c
+        lax.fori_loop(0, HEADS, fold, 0)
+        y = jnp.zeros((2 * HEADS, PAY), F32)
+        for xa in range(WIN):
+            hi, lo, _ = split3(folded[:, xa, :])
+            y = y + nt(jnp.concatenate([hi, lo], axis=0), fold_matrix(places[...], xa))
+        y = y[:HEADS] + y[HEADS:]
+        for t in range(2):
+            sums[l, t, :12, :PAY] = y[t * 12:(t + 1) * 12]
+        for n, j in ((0, 0), (1, 2)):
+            y = jnp.sum(dqkv[j].astype(F32), axis=0, keepdims=True)
+            for t in range(2):
+                sums[l, t, 12 + n:13 + n, :UC] = y[:, t * UC:(t + 1) * UC]
+        loads[4].wait()
+        emt[...] = n1[...].T
+        for j in range(3):
+            step_unit(l, 9 + j)
+            for t in range(2):
+                cols = slice(t * UC, (t + 1) * UC)
+                y = nt(dqkv[j, :, cols], w2d(wbuf, (9 + j) % 2, t))
+                if j == 0 and t == 0:
+                    acc[...] = y
+                else:
+                    acc[...] += y
+                emit(l, 9 + j, t, nn(emt[...], dqkv[j, :, cols]))
+        acc[...] = nn(permt[l], acc[...].astype(BF))
+        loads[5].wait()
+
+        def ln1(i):
+            r = pl.ds(i * WT, WT)
+            grad, gsum, bsum = norm_back(xb[0, r], acc[r], vec[pl.ds(l * 6, 1)])
+            e[r] += grad
+            sums[l, 2, 0:1] += gsum
+            sums[l, 2, 2:3] += bsum
+        rows_loop(4, ln1)
+        return carry
+    lax.fori_loop(0, LAYERS, layer, 0)
+    em[...] = e[...].astype(BF)
+    grad_swap = pltpu.make_async_remote_copy(
+        src_ref=em.at[theirs], dst_ref=gin, send_sem=xsend.at[1], recv_sem=xrecv.at[1],
+        device_id=at.side(at.x_side), device_id_type=MESH)
+    grad_swap.start()
+    gt[t_here] = e[mine]
+
+    def small_copy(n, src, dst, device):
+        return pltpu.make_async_remote_copy(src_ref=src, dst_ref=dst, send_sem=ssend.at[n], recv_sem=srecv.at[n],
+                                            device_id=device, device_id_type=MESH)
+    c = at.c
+    core_swap = small_copy(0, sums.at[1 - c], sm_core, at.sibling())
+    core_swap.start()
+    base = LAYERS * VIRT
+    rs.tick(base)
+    core_swap.wait_recv()
+    for n in range(3):
+        sums[c, n] += sm_core[n]
+    x_swaps = [small_copy(1, sums.at[c, 1 - t_here], sm_x.at[0], at.side(at.x_side)),
+               small_copy(2, sums.at[c, 2], sm_x.at[1], at.side(at.x_side))]
+    for cp in x_swaps:
+        cp.start()
+    rs.tick(base + 1)
+    for cp in x_swaps:
+        cp.wait_recv()
+    sm_y[0, 0] = sums[c, t_here] + sm_x[0]
+    sm_y[0, 1] = sums[c, 2] + sm_x[1]
+    y_swap = small_copy(3, sm_y.at[0], sm_y.at[1], at.side(at.y_side))
+    y_swap.start()
+    rs.tick(base + 2)
+    y_swap.wait_recv()
+    sm_z[at.z] = sm_y[0] + sm_y[1]
+    z_swaps = [small_copy(3 + k, sm_z.at[at.z], sm_z.at[at.z], at.above(k)) for k in (1, 2, 3)]
+    for cp in z_swaps:
+        cp.start()
+    rs.tick(base + 3)
+    for cp in z_swaps:
+        cp.wait_recv()
+    small[c] = (sm_z[0] + sm_z[1]) + (sm_z[2] + sm_z[3])
+    last = small_copy(7, small.at[c], small.at[c], at.sibling())
+    last.start()
+    grad_swap.wait()
+    gt[1 - t_here] = gin[...].astype(F32)
+    for n in range(4, REDUCE_LAGS[-1]):
+        rs.tick(base + n)
+    last.wait()
+    for cp in [core_swap, y_swap] + x_swaps + z_swaps:
+        cp.wait_send()
+    block_swap.wait()
+    block_keep.wait()
+
+
+def backward_call(cot, valid, vec, block, w, *saved):
+    perm = perm_matrices()
+    permt = jnp.asarray(perm.transpose(0, 2, 1), BF)
+    return pl.pallas_call(
+        backward_kernel,
+        out_shape=[sds((2, HALF, D), F32), sds((2, HALF, D), BF), sds((LAYERS * VIRT, 48, UC), F32),
+                   sds((LAYERS, 2, 16, D), F32)],
+        in_specs=[VM, SM, VM, VM, VM, VM, AN, AN] + [AN] * 8,
+        out_specs=[VM, AN, VM, VM],
+        scratch_shapes=[
+            pltpu.VMEM((TOK, D), F32), pltpu.VMEM((LAYERS, 3, 16, D), F32), pltpu.VMEM((HEADS, WIN, UC), F32),
+            pltpu.VMEM((HEADS, WT, UC), F32), pltpu.VMEM((3, 16, D), F32), pltpu.VMEM((2, 16, D), F32),
+            pltpu.VMEM((2, 2, 16, D), F32), pltpu.VMEM((4, 2, 16, D), F32), pltpu.VMEM((HALF, D), BF),
+            pltpu.VMEM((2, 2, 4, 2, 2, 48, UC), BF),
+            pltpu.VMEM((2, TOK, D), F32), pltpu.VMEM((TOK, D), BF), pltpu.VMEM((TOK, D), BF),
+            pltpu.VMEM((3, TOK, D), BF), pltpu.VMEM((TOK, D), BF), pltpu.VMEM((TOK, D), BF),
+            pltpu.VMEM((3, TOK, D), BF), pltpu.VMEM((TOK, D), F32), pltpu.VMEM((TOK, D), BF),
+            pltpu.VMEM((D, TOK), BF), pltpu.VMEM((D, TOK), BF), pltpu.VMEM((2, HG, WT, WT), BF),
+            pltpu.VMEM((2, 2, TOK, UC), BF), pltpu.VMEM((TOK, UC), F32), pltpu.VMEM((2, TOK, UC), BF),
+            pltpu.VMEM((REDUCE_SLOTS, 2, 4, 2, 2, 48, UC), BF),
+            pltpu.VMEM((REDUCE_SLOTS, 2, 4, 2, 48, UC), BF), pltpu.VMEM((REDUCE_SLOTS, 2, 4, 48, UC), BF),
+            pltpu.VMEM((REDUCE_SLOTS, 4, 48, UC), BF), pltpu.VMEM((REDUCE_SLOTS, 3, 48, UC), BF),
+            pltpu.SemaphoreType.DMA((2,)), pltpu.SemaphoreType.DMA((6,)),
+            pltpu.SemaphoreType.DMA((2,)), pltpu.SemaphoreType.DMA((2,)),
+            pltpu.SemaphoreType.DMA((REDUCE_SLOTS, 7)), pltpu.SemaphoreType.DMA((REDUCE_SLOTS, 7)),
+            pltpu.SemaphoreType.DMA((2,)), pltpu.SemaphoreType.DMA((2,)), pltpu.SemaphoreType.DMA((1,)),
+            pltpu.SemaphoreType.DMA((8,)), pltpu.SemaphoreType.DMA((8,)),
+        ],
+        compiler_params=pltpu.CompilerParams(vmem_limit_bytes=62 * 2**20, collective_id=1, has_side_effects=True),
+        name="backward",
+    )(cot, valid, vec, fold_places(), jnp.asarray(perm, BF), permt, block, w, *saved)
 
 
 def layer_norm(values, row_gain, row_shift):
@@ -48,7 +871,7 @@
     return image_grid.reshape((SIDE * SIDE, slot_count) + trailing)
 
 
-def shift_mask():
+def plan_mask():
     places = jnp.arange(SIDE, dtype=jnp.int32)
     band_of = (places >= SIDE - WIN).astype(jnp.int32) + (places >= SIDE - SHIFT).astype(jnp.int32)
     region = band_of[:, None] * 3 + band_of[None, :]
@@ -179,7 +1002,7 @@
         ).reshape(head_shape)
         bias_add = table_bias(rel_table[layer_index])[None]
         if shifted:
-            bias_add = bias_add + shift_mask()[:, None]
+            bias_add = bias_add + plan_mask()[:, None]
         blended, log_total = lax.map(
             lambda pieces: attend_image(pieces, bias_add, scale_factor),
             (queries, key_rows, value_rows),
@@ -372,9 +1195,52 @@
     )
 
 
+def unit_stack(w_qkv, w_proj, w_fc1, w_fc2):
+    layers, rows = w_qkv.shape[:2]
+    qkv = jnp.transpose(w_qkv, (0, 2, 1, 3))
+    proj = jnp.swapaxes(w_proj, 1, 2)[:, None]
+    fc1 = jnp.transpose(w_fc1.reshape(layers, rows, 4, UC), (0, 2, 1, 3))
+    fc2 = jnp.transpose(w_fc2.reshape(layers, 4, UC, rows), (0, 1, 3, 2))
+    ff = jnp.stack([fc1, fc2], axis=2).reshape(layers, 8, rows, UC)
+    return jnp.concatenate([qkv, proj, ff], axis=1).reshape(layers * NU, rows, UC)
+
+
+def unit_split(units):
+    rows = units.shape[1]
+    units = units.reshape(LAYERS, VIRT, rows, UC)[::-1]
+    back = [p if p < GAP[0] else p + GAP[1] - GAP[0] for p in range(NU)]
+    units = jnp.stack([units[:, back[BACK_ORDER.index(u)]] for u in range(NU)], axis=1)
+    qkv = jnp.transpose(units[:, :3], (0, 2, 1, 3))
+    proj = jnp.swapaxes(units[:, 3], 1, 2)
+    ff = units[:, 4:].reshape(LAYERS, 4, 2, rows, UC)
+    fc1 = jnp.transpose(ff[:, :, 0], (0, 2, 1, 3)).reshape(LAYERS, rows, 4 * UC)
+    fc2 = jnp.transpose(ff[:, :, 1], (0, 1, 3, 2)).reshape(LAYERS, 4 * UC, rows)
+    return qkv, proj, fc1, fc2
+
+
+def image_shards(tokens, valid, cotangent, row_gain, row_bias, w_qkv, qv_bias, w_proj, w_fc1, fc1_bias, w_fc2, rel_table):
+    t, d = lax.axis_index("tensor"), lax.axis_index("dp")
+    here = lax.dynamic_slice(valid, (t,), (1,))
+    shard = unit_stack(w_qkv, w_proj, w_fc1, w_fc2)
+    vecs = jnp.concatenate([row_gain, row_bias], axis=1).reshape(LAYERS * 6, 48)
+    vshard = jnp.pad(vecs.T, ((0, 0), (0, 128 - LAYERS * 6)))[None]
+    rows = jnp.concatenate([qv_bias.reshape(2 * LAYERS, UC), fc1_bias.reshape(4 * LAYERS, UC)]).astype(F32)
+    pay = jnp.concatenate([jnp.pad(rows, ((0, 4), (0, PAY - UC))),
+                           jnp.pad(rel_table.reshape(LAYERS * 12, RELS), ((0, 0), (0, PAY - RELS)))])
+    block, vec, cot, w, *saved = forward_call(
+        jnp.swapaxes(tokens, 0, 1), jnp.swapaxes(cotangent, 0, 1), here, vshard, pay, shard)
+    gt, block, total, small = backward_call(cot, here, vec, block, w, *saved)
+    qkv_g, proj_g, fc1_g, fc2_g = unit_split(total)
+    rowg = lax.dynamic_slice(small[:, 1], (0, 0, d * 48), (LAYERS, 6, 48))
+    own = small[:, 0]
+    return (jnp.swapaxes(block, 0, 1), jnp.swapaxes(gt, 0, 1), rowg[:, :2], rowg[:, 2:], qkv_g, own[:, 12:14, :UC],
+            proj_g, fc1_g, own[:, 14:16].reshape(LAYERS, 4 * UC), fc2_g, own[:, :12, :RELS])
+
+
 def solution(mesh):
+    whole_images = mesh.shape["tensor"] == 2 and mesh.shape["dp"] == 16
     return jax.shard_map(
-        shards,
+        image_shards if whole_images else shards,
         mesh=mesh,
         in_specs=(
             P("tensor", "dp", None),

time: 2050 us -> 535 us (0.26)
  waiting for transfers between devices: 1010 us -> 0 us
  Pallas kernels: 0 us -> 506 us
  local copies, waits for them, and re-layouts: 464 us -> 19.8 us
  matrix products: 249 us -> 0 us
  other arithmetic: 160 us -> 3.59 us
  blocking collectives: 135 us -> 0 us
    pallas_call x0 -> x2, Pallas kernels: none -> 506 us  [the longest x1 287 us: backward_call(): pl.pallas_call(backward_kernel, out_shape=[sds((2, HALF, D), F32), sds((2...]
    reduce_scatter x16 -> x0, waiting for transfers between devices: 428 us -> none  [the longest x2 115 us: shards(): lax.psum_scatter(proj_grad.astype(jnp.bfloat16), 'dp', scatter_dimension=...]
    all_gather x14 -> x0, waiting for transfers between devices: 287 us -> none  [the longest x2 77.1 us: shards(): lax.all_gather(w_fc1[layer_index], 'dp', axis=0, tiled=True)]
    dot_general x60 -> x0, matrix products: 249 us -> none  [the longest x4 31.3 us: table_back(): jnp.einsum('acr,bds,habcd->hrs', one_hot, one_hot, shaped, precision=lax....]
    unnamed x39 -> x0, waiting for transfers between devices: 210 us -> none
    another operation x52 -> x2, local copies, waits for them, and re-layouts: 136 us -> 0.09 us  [the longest x1 0.08 us: unit_stack(): ff = jnp.stack([fc1, fc2], axis=2).reshape(layers, 8, rows, UC)]
    all_gather x6 -> x0, blocking collectives: 126 us -> none  [the longest x2 44.6 us: shards(): lax.all_gather(row_gain[layer_index], 'dp', axis=1, tiled=True)]
    while x101 -> x0, local copies, waits for them, and re-layouts: 107 us -> none  [the longest x7 54 us: shards(): lax.map(lambda pieces: attend_back(pieces, bias_add, scale_factor), (quer...]
  transfers between devices with their start and end apart: 35 -> 0, of which waited for: 27 -> 0; matrix products, arithmetic and copies ran while one was open for 21% -> 0% of each run, Pallas kernels for 0% -> 0%
where the time goes in v1:
time: 535 us; the launch traced here: 531 us
  Pallas kernels  506 us (95%)
  local copies, waits for them, and re-layouts  19.8 us (4%)
    pallas_call x1, Pallas kernels, backward_call(): pl.pallas_call(backward_kernel, out_shape=[sds((2, HALF, D), F32), sds((2...  287 us
    pallas_call x1, Pallas kernels, forward_call(): pl.pallas_call(forward_kernel, out_shape=[sds((TOK, D), BF), sds((16, D),...  219 us

profile of v1, /device:TPU:0, one launch (start us, length us, event | category | flops | bytes accessed | tf_op | source)
XLA Modules:
  0.0 530.7 jit_solution(11725065054968448385)
XLA Ops:
  0.6 0.0 copy-start.4
  0.7 1.3 dynamic_slice.8.valid
  1.9 0.7 reshape.63
  2.6 0.7 pad_maximum_fusion.2
  3.4 0.7 reshape.64
  4.1 0.1 copy.44
  4.2 0.6 pad_bitcast_fusion.vshard
  4.8 0.8 copy.45
  5.6 0.7 select_maximum_fusion.pay
  6.3 1.0 reshape.66
  7.3 0.0 copy-done.4
  7.3 0.1 reshape.67
  7.4 0.0 copy-start.5
  7.4 0.0 copy-start.7
  7.4 0.4 pad_maximum_fusion.1
  7.9 0.1 copy.46
  8.0 0.0 copy-start.2
  8.0 0.0 copy-start.3
  8.0 0.4 copy-done.5
  8.4 0.1 copy-done.7
  8.4 1.0 pad_maximum_fusion
  9.4 0.0 copy-done.2
  9.4 0.0 copy-done.3
  9.4 1.4 copy_bitcast_fusion
  10.9 219.0 %forward.1 = (bf16[576,768]{1,0:T(8,128)(2,1)}, f32[16,768]{1,0:T(8,128)}, bf16[576,768]{1,0:T(8,128)(2,1)}, bf16[24,2,4,2,2,48,384]{6,5,4,3,2,1,0:T(8,128)(2,1)...) custom-call(bf16[2,288,768]{2,1,0:T(8,128)(2,1)} %get-tuple-element., ...), custom_call_target="tpu_custom_call" | custom-call | tf_op jit(solution)/shard_map/forward/pallas_call | solution.py:431
  229.8 287.1 %backward.1 = (f32[2,288,768]{2,1,0:T(8,128)}, bf16[2,288,768]{2,1,0:T(8,128)(2,1)}, f32[32,48,384]{2,1,0:T(8,128)}, f32[2,2,16,768]{3,2,1,0:T(8,128)}) custom-call(bf16[576,768]{1,0:T(8,128)(2,1)} %get-tuple-element.27.cot, s32[1]{0:T(128)} %dynamic_slice.8.valid, f32[16,768]{1,0:T(8,128)} %get-tuple-element.28.vec, s32[1,384]{1,0:T(1,128)} %constant.32.clone.places, ...), custom_call_target="tpu_custom_call" | custom-call | tf_op jit(solution)/shard_map/backward/pallas_call | solution.py:811
  516.9 0.0 copy-start
  516.9 3.1 copy.51
  520.1 0.0 copy-done
  520.1 0.0 copy-start.6
  520.1 0.0 copy-start.1
  520.1 2.6 copy.52
  522.6 0.0 copy-done.6
  522.7 0.1 dynamic-slice_bitcast_fusion
  522.7 0.6 slice.136
  523.3 0.6 slice.137
  523.9 0.6 slice.141
  524.5 0.7 copy.53
  525.2 0.6 copy.57
  525.8 0.0 copy-done.1
  525.8 0.1 fusion.7
  526.0 0.7 reverse_bitcast_fusion
  526.7 0.8 maximum_bitcast_fusion
  527.6 0.1 fusion.8
  527.7 0.2 copy.62
  527.9 1.1 reshape.74
  529.0 0.2 copy.63
  529.2 1.1 reshape.72
  (17 shorter events, 0.2 us)
Async XLA Ops:
  0.6 6.7 %copy-start.4 = (bf16[2,1536,48]{1,2,0:T(8,128)(2,1)S(1)}, bf16[2,1536,48]{1,2,0:T(8,128)(2,1)}, u32[]{:S(2)}) copy-start(bf16[2,1536,48]{1,2,0:T(8,128)(2,1)} %param.29) | copy-start | bytes 884740
  7.4 0.9 copy-start.5
  7.4 1.0 copy-start.7
  8.0 1.5 copy-start.2
  8.0 1.5 copy-start.3
  516.9 3.1 copy-start
  520.1 2.6 copy-start.6
  520.1 5.7 %copy-start.1 = (f32[32,48,384]{2,1,0:T(8,128)S(1)}, f32[32,48,384]{2,1,0:T(8,128)}, u32[]{:S(2)}) copy-start(f32[32,48,384]{2,1,0:T(8,128)} %get-tuple-element.42) | copy-start | bytes 7077892

commit v2 on v1

--- a/solution.py
+++ b/solution.py
@@ -75,7 +75,7 @@
     region = region.reshape(2, WIN, 2, WIN).transpose(0, 2, 1, 3).reshape(4, WT)
     same = region[:, :, None] == region[:, None, :]
     masked = np.where(same, 0.0, MASK_FILL).astype(np.float32)
-    return np.stack([np.zeros_like(masked), masked])
+    return np.tile(np.stack([np.zeros_like(masked), masked]), (1, 1, 1, HG))
 
 
 def rows_loop(n, body):
@@ -85,8 +85,22 @@
     lax.fori_loop(0, n, step, 0)
 
 
-def w2d(wbuf, slot, t):
-    return wbuf[slot, t].reshape(D, UC)
+def w2d(wbuf, slot):
+    return wbuf[slot].reshape(D, 2 * UC)
+
+
+class Fetch:
+    def __init__(self, w_hbm, wbuf, sem, g, slot):
+        self.copies = [pltpu.make_async_copy(w_hbm.at[g, t], wbuf.at[slot, :, :, :, :, t * UC:(t + 1) * UC], sem.at[slot, t])
+                       for t in range(2)]
+
+    def start(self):
+        for cp in self.copies:
+            cp.start()
+
+    def wait(self):
+        for cp in self.copies:
+            cp.wait()
 
 
 class Place:
@@ -125,9 +139,9 @@
 
 
 MESH = pl.DeviceIdType.MESH
-GATHER_LAGS = (1, 2, 3, 4)
-GATHER_SEMS = 8
-TICK_EVERY = 4
+GATHER_LAGS = (2, 4, 6, 7)
+GATHER_SEMS = 12
+TICK_EVERY = 6
 
 
 class Gather:
@@ -207,13 +221,13 @@
 
 def fold_places():
     lane = np.arange(UC)
-    j, xb = lane // WIN, lane % WIN
-    return np.where(j < 2 * WIN - 1, (2 * WIN - 2 - j) * (2 * WIN - 1) - xb + WIN - 1, -4 * PAY).astype(np.int32)[None]
-
-
-def fold_matrix(places, xa):
+    j, xa = lane // WIN, lane % WIN
+    return np.where(j < 2 * WIN - 1, j * (2 * WIN - 1) + xa + WIN - 1, -4 * PAY).astype(np.int32)[None]
+
+
+def fold_matrix(places, xb):
     rows = lax.broadcasted_iota(jnp.int32, (PAY, UC), 0)
-    return jnp.where(rows == places + xa, 1.0, 0.0).astype(BF)
+    return jnp.where(rows == places - xb, 1.0, 0.0).astype(BF)
 
 
 def split3(x):
@@ -223,6 +237,18 @@
     return hi, mid, (rest - mid.astype(F32)).astype(BF)
 
 
+HT = HG * WT
+CHUNKS = [slice(i, min(i + 128, HT)) for i in range(0, HT, 128)]
+
+
+def by_head(x, lanes):
+    return jnp.concatenate([jnp.where(lanes == h, x, jnp.zeros_like(x)) for h in range(HG)], axis=0)
+
+
+def own_blocks(x):
+    return jnp.concatenate([x[h * HDIM:(h + 1) * HDIM, h * WT:(h + 1) * WT] for h in range(HG)], axis=0).T
+
+
 def half_rows(t):
     return pl.ds(pl.multiple_of(t * HALF, HALF), HALF)
 
@@ -230,7 +256,7 @@
 def forward_kernel(tok, cot, valid, vshard, pay, places, mask, perm, permt, shard,
                    out, vec, cot_h, w_hbm, x0_h, x1_h, n1_h, qkv_h, pw_h, o_h, n2_h, gg_h,
                    wbuf, x0, x1, n1, qkv, ow, n2, acc, pst, gst, ubuf,
-                   xin, vall, pays, ext, bias,
+                   xin, vall, pays, ext, bias, scores,
                    wsem, ssem, psem, gsem, gsend, grecv, glocal, vsend, vrecv, vlocal, xsend, xrecv, xlocal):
     at = Place()
     ag = Gather(at, shard, w_hbm, gsend, grecv, glocal, LAYERS * NU)
@@ -262,27 +288,27 @@
             for xa in range(WIN):
                 y = nn(parts, fold_matrix(places[...], xa))
                 ext[:, xa, :] = y[:48] + y[48:96] + y[96:]
-    for n in range(2, 3):
-        swaps[n].start()
-        keeps[n].start()
-
     def spread(i, c):
-        half, l, h = lax.div(i, 24), lax.rem(lax.div(i, 12), 2), lax.rem(i, 12)
-        x = ext[i]
-        for ya in range(WIN):
-            off = (WIN - 1 - ya) * WIN
-            bias[l, half * 12 + h, ya * WIN:(ya + 1) * WIN, :] = x[:, off:off + WT]
+        half, l, g = lax.div(i, 6), lax.rem(lax.div(i, 3), 2), lax.rem(i, 3)
+        for h in range(HG):
+            x = ext[half * 24 + l * 12 + g * HG + h]
+            for yb in range(WIN):
+                off = (WIN - 1 - yb) * WIN
+                bias[l, half * 3 + g, yb * WIN:(yb + 1) * WIN, h * WT:(h + 1) * WT] = x[:, off:off + WT]
         return c
-    lax.fori_loop(0, 48, spread, 0)
+    lax.fori_loop(0, 12, spread, 0)
     vec[...] = vall[0, 0].reshape(D, 128).astype(F32).T[:16]
     swaps[0].wait()
     keeps[0].wait()
 
+    def both(row):
+        return jnp.concatenate([pays[0, pl.ds(row, 1), :UC], pays[1, pl.ds(row, 1), :UC]], axis=1)
+
     def vrow(l, i):
         return vec[pl.ds(l * 6 + i, 1)]
 
     def fetch(g, u):
-        return pltpu.make_async_copy(w_hbm.at[g], wbuf.at[u % 2], wsem.at[u % 2])
+        return Fetch(w_hbm, wbuf, wsem, g, u % 2)
 
     def tick_base(l, u):
         inside = 4 * NG // TICK_EVERY
@@ -312,14 +338,10 @@
         n1_l[...] = nn(perm[l], ow_l[...]).astype(BF)
         for j in range(3):
             step_unit(l, j)
-            for t in range(2):
-                cols = slice(t * UC, (t + 1) * UC)
-                y = nn(n1_l[...], w2d(wbuf, j % 2, t))
-                if j == 0:
-                    y = y + pays[t, pl.ds(l * 2, 1), :UC]
-                if j == 2:
-                    y = y + pays[t, pl.ds(l * 2 + 1, 1), :UC]
-                qkv[l, j, :, cols] = y.astype(BF)
+            y = nn(n1_l[...], w2d(wbuf, j % 2))
+            if j != 1:
+                y = y + both(l * 2 + j // 2)
+            qkv[l, j] = y.astype(BF)
 
         def attend(it, c):
             w, hg = lax.div(it, NG), lax.rem(it, NG)
@@ -327,20 +349,17 @@
             cl = pl.ds(pl.multiple_of(hg * 128, 128), 128)
             slot = lax.rem(it, 2)
             q, k, v = qkv[l, 0, r, cl], qkv[l, 1, r, cl], qkv[l, 2, r, cl]
-            put = pltpu.make_async_copy(pst.at[slot], pw_h.at[l, w, pl.ds(hg * HG, HG)], psem.at[slot])
+            put = pltpu.make_async_copy(pst.at[slot], pw_h.at[l, w, hg], psem.at[slot])
 
             @pl.when((it >= 2) | (l > 0))
             def _():
                 put.wait()
-            o = jnp.zeros((WT, 128), F32)
-            for h in range(HG):
-                qm = jnp.where(lanes == h, q, jnp.zeros_like(q))
-                s = nt(qm, k) * SCALE + bias[l, hg * HG + h] + mask[l, w]
-                e = jnp.exp(s - jnp.max(s, axis=-1, keepdims=True))
-                p = (e * (1.0 / jnp.sum(e, axis=-1, keepdims=True))).astype(BF)
-                pst[slot, h] = p
-                o = jnp.where(lanes == h, nn(p, v), o)
-            ow_l[r, cl] = o.astype(BF)
+            scores[...] = nt(k, by_head(q, lanes))
+            for ch in CHUNKS:
+                x = scores[:, ch] * SCALE + bias[l, hg, :, ch] + mask[l, w, :, ch]
+                x = jnp.exp(x - jnp.max(x, axis=0, keepdims=True))
+                pst[slot, :, ch] = (x * (1.0 / jnp.sum(x, axis=0, keepdims=True))).astype(BF)
+            ow_l[r, cl] = own_blocks(nn(v.T, pst[slot])).astype(BF)
             put.start()
 
             @pl.when(lax.rem(it, TICK_EVERY) == TICK_EVERY - 1)
@@ -348,14 +367,14 @@
                 ag.tick(tick_base(l, 3) + lax.div(it, TICK_EVERY))
             return c
         lax.fori_loop(0, 4 * NG, attend, 0)
+
+        @pl.when(l == LAYERS - 1)
+        def _():
+            swaps[2].start()
+            keeps[2].start()
         n2_l[...] = nn(permt[l], ow_l[...]).astype(BF)
         step_unit(l, 3)
-        for t in range(2):
-            y = nt(n2_l[:, t * UC:(t + 1) * UC], w2d(wbuf, 1, t))
-            if t == 0:
-                acc[...] = y
-            else:
-                acc[...] += y
+        acc[...] = nt(n2_l[...], w2d(wbuf, 1))
 
         def ln2(i):
             r = pl.ds(i * WT, WT)
@@ -367,26 +386,24 @@
         rows_loop(4, ln2)
         for i in range(4):
             step_unit(l, 4 + 2 * i)
-            for t in range(2):
-                put = pltpu.make_async_copy(gst.at[t], gg_h.at[l, i, t], gsem.at[t])
-                if i > 0:
+            put = pltpu.make_async_copy(gst.at[i % 2], gg_h.at[l, i], gsem.at[i % 2])
+            if i > 1:
+                put.wait()
+            else:
+                @pl.when(l > 0)
+                def _():
                     put.wait()
-                else:
-                    @pl.when(l > 0)
-                    def _():
-                        put.wait()
-                ubuf[...] = nn(n2_l[...], w2d(wbuf, 0, t)) + pays[t, pl.ds(4 + l * 4 + i, 1), :UC]
-
-                def act(n):
-                    r = pl.ds(n * 96, 96)
-                    g, gp = gelu_parts(ubuf[r])
-                    gst[t, 0, r] = g.astype(BF)
-                    gst[t, 1, r] = gp.astype(BF)
-                rows_loop(6, act)
-                put.start()
+            ubuf[...] = nn(n2_l[...], w2d(wbuf, 0)) + both(4 + l * 4 + i)
+
+            def act(n):
+                r = pl.ds(n * 48, 48)
+                g, gp = gelu_parts(ubuf[r])
+                gst[i % 2, 0, r] = g.astype(BF)
+                gst[i % 2, 1, r] = gp.astype(BF)
+            rows_loop(12, act)
+            put.start()
             step_unit(l, 5 + 2 * i)
-            for t in range(2):
-                acc[...] += nt(gst[t, 0], w2d(wbuf, 1, t))
+            acc[...] += nt(gst[i % 2, 0], w2d(wbuf, 1))
 
         for ref, dst in ((x0, x0_h), (x1, x1_h), (n1, n1_h), (qkv, qkv_h), (ow, o_h), (n2, n2_h)):
             pltpu.make_async_copy(ref.at[l], dst.at[l], ssem.at[l]).start()
@@ -404,8 +421,8 @@
         for ref, dst in ((x0, x0_h), (x1, x1_h), (n1, n1_h), (qkv, qkv_h), (ow, o_h), (n2, n2_h)):
             pltpu.make_async_copy(ref.at[l], dst.at[l], ssem.at[l]).wait()
     for s in range(2):
-        pltpu.make_async_copy(pst.at[s], pw_h.at[0, 0, pl.ds(0, HG)], psem.at[s]).wait()
-        pltpu.make_async_copy(gst.at[s], gg_h.at[0, 0, s], gsem.at[s]).wait()
+        pltpu.make_async_copy(pst.at[s], pw_h.at[0, 0, 0], psem.at[s]).wait()
+        pltpu.make_async_copy(gst.at[s], gg_h.at[0, s], gsem.at[s]).wait()
     swaps[2].wait()
     keeps[2].wait()
 
@@ -420,8 +437,8 @@
 
 SAVED = [
     sds((LAYERS, TOK, D), F32), sds((LAYERS, TOK, D), F32), sds((LAYERS, TOK, D), BF),
-    sds((LAYERS, 3, TOK, D), BF), sds((LAYERS, 4, HEADS, WT, WT), BF),
-    sds((LAYERS, TOK, D), BF), sds((LAYERS, TOK, D), BF), sds((LAYERS, 4, 2, 2, TOK, UC), BF),
+    sds((LAYERS, 3, TOK, D), BF), sds((LAYERS, 4, NG, WT, HT), BF),
+    sds((LAYERS, TOK, D), BF), sds((LAYERS, TOK, D), BF), sds((LAYERS, 4, 2, TOK, 2 * UC), BF),
 ]
 
 
@@ -435,16 +452,16 @@
         in_specs=[AN, AN, SM, AN, AN, VM, VM, VM, VM, AN],
         out_specs=[VM, VM] + [AN] * 10,
         scratch_shapes=[
-            pltpu.VMEM((2, 2, 4, 2, 2, 48, UC), BF),
+            pltpu.VMEM((2, 4, 2, 2, 48, 2 * UC), BF),
             pltpu.VMEM((2, TOK, D), F32), pltpu.VMEM((2, TOK, D), F32),
             pltpu.VMEM((2, TOK, D), BF), pltpu.VMEM((2, 3, TOK, D), BF),
             pltpu.VMEM((2, TOK, D), BF), pltpu.VMEM((2, TOK, D), BF),
-            pltpu.VMEM((TOK, D), F32), pltpu.VMEM((2, HG, WT, WT), BF),
-            pltpu.VMEM((2, 2, TOK, UC), BF), pltpu.VMEM((TOK, UC), F32),
+            pltpu.VMEM((TOK, D), F32), pltpu.VMEM((2, WT, HT), BF),
+            pltpu.VMEM((2, 2, TOK, 2 * UC), BF), pltpu.VMEM((TOK, 2 * UC), F32),
             pltpu.VMEM((TOK, D), BF), pltpu.VMEM((1, 2, 4, 2, 2, 48, 128), BF),
             pltpu.VMEM((2, 40, PAY), F32), pltpu.VMEM((48, WIN, UC), F32),
-            pltpu.VMEM((LAYERS, HEADS, WT, WT), F32),
-            pltpu.SemaphoreType.DMA((2,)), pltpu.SemaphoreType.DMA((2,)),
+            pltpu.VMEM((LAYERS, NG, WT, HT), F32), pltpu.VMEM((WT, HT), F32),
+            pltpu.SemaphoreType.DMA((2, 2)), pltpu.SemaphoreType.DMA((2,)),
             pltpu.SemaphoreType.DMA((2,)), pltpu.SemaphoreType.DMA((2,)),
             pltpu.SemaphoreType.DMA((GATHER_SEMS, 7)), pltpu.SemaphoreType.DMA((GATHER_SEMS, 7)),
             pltpu.SemaphoreType.DMA((GATHER_SEMS,)),
@@ -467,12 +484,13 @@
     return grad, jnp.sum(dn * xh, axis=0, keepdims=True), jnp.sum(dn, axis=0, keepdims=True)
 
 
-REDUCE_SLOTS = 8
+REDUCE_SLOTS = NU
+CORE_SLOTS = 4
 PAY = 640
 HALF = TOK // 2
-VIRT = 16
-GAP = (9, 13)
-REDUCE_LAGS = (1, 2, 3, 4)
+VIRT = 18
+GAP = (9, 15)
+REDUCE_LAGS = (1, 5, 8, 11)
 
 
 class Reduce:
@@ -481,31 +499,43 @@
         self.core_in, self.first_in, self.second_in, self.z_in = core_in, first_in, second_in, z_in
         self.send, self.recv = send, recv
 
+    def slot(self, v):
+        place = lax.rem(v, VIRT)
+        return jnp.where(place < GAP[0], place, place - (GAP[1] - GAP[0]))
+
     def copy(self, v, n, src, dst, device):
-        slot = lax.rem(v, REDUCE_SLOTS)
+        slot = self.slot(v)
         return pltpu.make_async_remote_copy(
             src_ref=src, dst_ref=dst, send_sem=self.send.at[slot, n], recv_sem=self.recv.at[slot, n],
             device_id=device, device_id_type=MESH)
 
     def core(self, v):
-        slot = lax.rem(v, REDUCE_SLOTS)
-        return self.copy(v, 0, self.own.at[slot, :, :, :, 1 - self.at.c], self.core_in.at[slot], self.at.sibling())
+        slot = lax.rem(self.slot(v), CORE_SLOTS)
+        return self.copy(v, 0, self.own.at[REDUCE_SLOTS + slot], self.core_in.at[slot], self.at.sibling())
+
+    def put(self, v, value):
+        value = value.astype(BF)
+        mine, other = self.slot(v), REDUCE_SLOTS + lax.rem(self.slot(v), CORE_SLOTS)
+        for t in range(2):
+            x = value[:, t * UC:(t + 1) * UC].reshape(4, 2, 2, 48, UC)
+            for k in range(2):
+                self.own[jnp.where(self.at.c == k, mine, other), t] = x[:, :, k]
 
     def group(self, v, ty):
-        return self.own.at[lax.rem(v, REDUCE_SLOTS), ty[0], :, ty[1], self.at.c]
+        return self.own.at[self.slot(v), ty[0], :, ty[1]]
 
     def first(self, v, n):
         p = self.at
         ty = p.diagonal if n == 0 else p.second
-        return self.copy(v, 1 + n, self.group(v, ty), self.first_in.at[lax.rem(v, REDUCE_SLOTS), n], p.side(p.second))
+        return self.copy(v, 1 + n, self.group(v, ty), self.first_in.at[self.slot(v), n], p.side(p.second))
 
     def second(self, v):
         p = self.at
-        return self.copy(v, 3, self.group(v, p.first), self.second_in.at[lax.rem(v, REDUCE_SLOTS)], p.side(p.first))
+        return self.copy(v, 3, self.group(v, p.first), self.second_in.at[self.slot(v)], p.side(p.first))
 
     def up(self, v, k):
-        p, slot = self.at, lax.rem(v, REDUCE_SLOTS)
-        return self.copy(v, 3 + k, self.own.at[slot, p.t, p.along(k), p.y, p.c], self.z_in.at[slot, k - 1], p.above(k))
+        p, slot = self.at, self.slot(v)
+        return self.copy(v, 3 + k, self.own.at[slot, p.t, p.along(k), p.y], self.z_in.at[slot, k - 1], p.above(k))
 
     def add(self, ref, other):
         def one(z):
@@ -513,15 +543,15 @@
         rows_loop(4, one)
 
     def stage(self, n, v):
-        p, slot = self.at, lax.rem(v, REDUCE_SLOTS)
+        p, slot = self.at, self.slot(v)
         if n == 0:
             self.core(v).start()
         elif n == 1:
-            self.core(v).wait_recv()
+            self.core(v).wait()
 
             def one(i):
                 t, z = lax.div(i, 4), lax.rem(i, 4)
-                self.own[slot, t, z, :, p.c] = self.own[slot, t, z, :, p.c] + self.core_in[slot, t, z]
+                self.own[slot, t, z] = self.own[slot, t, z] + self.core_in[lax.rem(self.slot(v), CORE_SLOTS), t, z]
             rows_loop(8, one)
             self.first(v, 0).start()
             self.first(v, 1).start()
@@ -537,12 +567,11 @@
             for k in (1, 2, 3):
                 self.up(v, k).start()
         else:
-            total = self.own[slot, p.t, p.z, p.y, p.c].astype(F32)
+            total = self.own[slot, p.t, p.z, p.y].astype(F32)
             for k in (1, 2, 3):
                 self.up(v, k).wait_recv()
                 total = total + self.z_in[slot, k - 1].astype(F32)
-            self.total[v] = total
-            self.core(v).wait_send()
+            self.total[lax.div(v, VIRT) * NU + slot] = total
             for n in range(2):
                 self.first(v, n).wait_send()
             self.second(v).wait_send()
@@ -561,7 +590,7 @@
 
 def backward_kernel(cot, valid, vec, places, perm, permt, block, w_hbm, x0_h, x1_h, n1_h, qkv_h, pw_h, o_h, n2_h, gg_h,
                     gt, block2, total, small,
-                    e, sums, folded, dsum, sm_core, sm_x, sm_y, sm_z, gin,
+                    e, scores, ds, sums, folded, dsum, sm_core, sm_x, sm_y, sm_z, gin,
                     wbuf, xb, n1, n2, qkv, ow, do, dqkv, acc, em, emt, n2t, pst, gst, ubuf, dub, gbuf,
                     core_in, first_in, second_in, z_in,
                     wsem, lsem, psem, gsem, rsend, rrecv, xsend, xrecv, xlocal, ssend, srecv):
@@ -571,7 +600,7 @@
     rs = Reduce(at, gbuf, core_in, first_in, second_in, z_in, total, rsend, rrecv)
 
     def fetch(g, pos):
-        return pltpu.make_async_copy(w_hbm.at[g], wbuf.at[pos % 2], wsem.at[pos % 2])
+        return Fetch(w_hbm, wbuf, wsem, g, pos % 2)
 
     def step_unit(l, pos):
         fetch(0, pos).wait()
@@ -585,11 +614,10 @@
     def place_of(pos):
         return pos if pos < GAP[0] else pos + GAP[1] - GAP[0]
 
-    def emit(l, pos, t, value):
-        v = place_of(pos)
-        gbuf[v % REDUCE_SLOTS, t] = value.astype(BF).reshape(4, 2, 2, 48, UC)
-        if t == 1:
-            rs.tick((LAYERS - 1 - l) * VIRT + v)
+    def emit(l, pos, value):
+        v = (LAYERS - 1 - l) * VIRT + place_of(pos)
+        rs.put(v, value)
+        rs.tick(v)
 
     fetch((LAYERS - 1) * NU + BACK_ORDER[0], 0).start()
     at.barrier()
@@ -612,7 +640,7 @@
             cp.start()
 
         def load_gg(k):
-            return pltpu.make_async_copy(gg_h.at[l, k // 2, k % 2], gst.at[k % 2], gsem.at[k % 2])
+            return pltpu.make_async_copy(gg_h.at[l, k], gst.at[k % 2], gsem.at[k % 2])
         load_gg(0).start()
         load_gg(1).start()
 
@@ -627,27 +655,27 @@
         n2t[...] = n2[...].T
         for i in range(4):
             step_unit(l, 2 * i)
+            load_gg(i).wait()
+            ubuf[...] = nn(em[...], w2d(wbuf, 0))
+
+            def act(n, c):
+                r = pl.ds(n * 48, 48)
+                du = (ubuf[r] * gst[i % 2, 1, r].astype(F32)).astype(BF)
+                dub[r] = du
+                return c + jnp.sum(du.astype(F32), axis=0, keepdims=True)
+            y = lax.fori_loop(0, 12, act, jnp.zeros((1, 2 * UC), F32))
             for t in range(2):
-                load_gg(2 * i + t).wait()
-                ubuf[...] = nn(em[...], w2d(wbuf, 0, t))
-
-                def act(n):
-                    r = pl.ds(n * 96, 96)
-                    du = (ubuf[r] * gst[t, 1, r].astype(F32)).astype(BF)
-                    dub[t, r] = du
-                    sums[l, t, 14 + i // 2:15 + i // 2, (i % 2) * UC:(i % 2 + 1) * UC] += jnp.sum(du.astype(F32), axis=0, keepdims=True)
-                rows_loop(6, act)
-                emit(l, 2 * i, t, nn(emt[...], gst[t, 0]))
-                if i < 3:
-                    load_gg(2 * i + t + 2).start()
+                sums[l, t, 14 + i // 2:15 + i // 2, (i % 2) * UC:(i % 2 + 1) * UC] = y[:, t * UC:(t + 1) * UC]
+            emit(l, 2 * i, nn(emt[...], gst[i % 2, 0]))
+            if i < 2:
+                load_gg(i + 2).start()
             step_unit(l, 2 * i + 1)
-            for t in range(2):
-                y = nt(dub[t], w2d(wbuf, 1, t))
-                if i == 0 and t == 0:
-                    acc[...] = y
-                else:
-                    acc[...] += y
-                emit(l, 2 * i + 1, t, nn(n2t[...], dub[t]))
+            y = nt(dub[...], w2d(wbuf, 1))
+            if i == 0:
+                acc[...] = y
+            else:
+                acc[...] += y
+            emit(l, 2 * i + 1, nn(n2t[...], dub[...]))
         loads[1].wait()
 
         def ln2(i):
@@ -664,17 +692,15 @@
         emt[...] = n2[...].T
         step_unit(l, 8)
         loads[2].wait()
-        for t in range(2):
-            cols = slice(t * UC, (t + 1) * UC)
-            do[:, cols] = nn(n2[...], w2d(wbuf, 0, t)).astype(BF)
-            emit(l, 8, t, nn(emt[...], ow[:, cols]))
+        do[...] = nn(n2[...], w2d(wbuf, 0)).astype(BF)
+        emit(l, 8, nn(emt[...], ow[...]))
         loads[3].wait()
 
         def load_pw(it):
             w, hg = lax.div(it, NG), lax.rem(it, NG)
-            return pltpu.make_async_copy(pw_h.at[l, w, pl.ds(hg * HG, HG)], pst.at[lax.rem(it, 2)], psem.at[lax.rem(it, 2)])
+            return pltpu.make_async_copy(pw_h.at[l, w, hg], pst.at[lax.rem(it, 2)], psem.at[lax.rem(it, 2)])
         load_pw(0).start()
-        dsum[...] = jnp.zeros_like(dsum)
+        dsum[l] = jnp.zeros((NG, WT, HT), F32)
 
         def attend(it, c):
             w, hg = lax.div(it, NG), lax.rem(it, NG)
@@ -686,45 +712,26 @@
             def _():
                 load_pw(it + 1).start()
             q, k, v, d = qkv[0, r, cl], qkv[1, r, cl], qkv[2, r, cl], do[r, cl]
-            qt, dt = q.T, d.T
+            q4, d4 = by_head(q, lanes), by_head(d, lanes)
+            scores[...] = nt(v, d4)
             load_pw(it).wait()
-            dq = jnp.zeros((WT, 128), F32)
-            dkt, dvt = [], []
-            for h in range(HG):
-                pw = pst[slot, h]
-                p = pw.astype(F32)
-                dp = nt(jnp.where(lanes == h, d, jnp.zeros_like(d)), v)
-                mean = jnp.sum(p * dp, axis=-1, keepdims=True) / jnp.sum(p, axis=-1, keepdims=True)
-                ds = (p * (dp - mean)).astype(BF)
-                dsum[hg * HG + h, :, :WT] += ds.astype(F32)
-                hr = slice(h * HDIM, (h + 1) * HDIM)
-                dvt.append(nn(dt[hr], pw))
-                dkt.append(nn(qt[hr], ds))
-                dq = jnp.where(lanes == h, nn(ds, k), dq)
-            dqkv[0, r, cl] = (dq * SCALE).astype(BF)
-            dqkv[1, r, cl] = (jnp.concatenate(dkt, axis=0) * SCALE).T.astype(BF)
-            dqkv[2, r, cl] = jnp.concatenate(dvt, axis=0).T.astype(BF)
-
-            @pl.when(lax.rem(it, 6) == 5)
+            for ch in CHUNKS:
+                p = pst[slot, :, ch].astype(F32)
+                x = scores[:, ch]
+                mean = jnp.sum(p * x, axis=0, keepdims=True) / jnp.sum(p, axis=0, keepdims=True)
+                x = (p * (x - mean)).astype(BF)
+                ds[:, ch] = x
+                dsum[l, hg, :, ch] += x.astype(F32)
+            dqkv[0, r, cl] = (own_blocks(nn(k.T, ds[...])) * SCALE).astype(BF)
+            dqkv[1, r, cl] = (nn(ds[...], q4) * SCALE).astype(BF)
+            dqkv[2, r, cl] = nn(pst[slot], d4).astype(BF)
+
+            @pl.when(lax.rem(it, 4) == 3)
             def _():
-                rs.tick(step * VIRT + GAP[0] + lax.div(it, 6))
+                rs.tick(step * VIRT + GAP[0] + lax.div(it, 4))
             return c
         lax.fori_loop(0, 4 * NG, attend, 0)
 
-        def fold(h, c):
-            x = jnp.zeros((WIN, UC), F32)
-            for ya in range(WIN):
-                x = x + pltpu.roll(dsum[h, ya * WIN:(ya + 1) * WIN, :], (WIN - 1 - ya) * WIN, 1)
-            folded[h] = x
-            return c
-        lax.fori_loop(0, HEADS, fold, 0)
-        y = jnp.zeros((2 * HEADS, PAY), F32)
-        for xa in range(WIN):
-            hi, lo, _ = split3(folded[:, xa, :])
-            y = y + nt(jnp.concatenate([hi, lo], axis=0), fold_matrix(places[...], xa))
-        y = y[:HEADS] + y[HEADS:]
-        for t in range(2):
-            sums[l, t, :12, :PAY] = y[t * 12:(t + 1) * 12]
         for n, j in ((0, 0), (1, 2)):
             y = jnp.sum(dqkv[j].astype(F32), axis=0, keepdims=True)
             for t in range(2):
@@ -733,14 +740,12 @@
         emt[...] = n1[...].T
         for j in range(3):
             step_unit(l, 9 + j)
-            for t in range(2):
-                cols = slice(t * UC, (t + 1) * UC)
-                y = nt(dqkv[j, :, cols], w2d(wbuf, (9 + j) % 2, t))
-                if j == 0 and t == 0:
-                    acc[...] = y
-                else:
-                    acc[...] += y
-                emit(l, 9 + j, t, nn(emt[...], dqkv[j, :, cols]))
+            y = nt(dqkv[j], w2d(wbuf, (9 + j) % 2))
+            if j == 0:
+                acc[...] = y
+            else:
+                acc[...] += y
+            emit(l, 9 + j, nn(emt[...], dqkv[j]))
         acc[...] = nn(permt[l], acc[...].astype(BF))
         loads[5].wait()
 
@@ -760,13 +765,38 @@
     grad_swap.start()
     gt[t_here] = e[mine]
 
+    base = LAYERS * VIRT
+
+    def fold(i, c):
+        for h in range(HG):
+            x = jnp.zeros((2 * WIN, UC), F32)
+            for pair in range(WIN // 2):
+                part = dsum[lax.div(i, NG), lax.rem(i, NG), 2 * pair * WIN:2 * (pair + 1) * WIN, h * WT:(h + 1) * WT]
+                part = jnp.concatenate([part, jnp.zeros((2 * WIN, UC - WT), F32)], axis=1)
+                x = x + pltpu.roll(part, (WIN - 1 - 2 * pair) * WIN, 1)
+            folded[i * HG + h] = x[:WIN] + pltpu.roll(x[WIN:], UC - WIN, 1)
+
+        @pl.when(lax.rem(i, 2) == 1)
+        def _():
+            rs.tick(base + lax.div(i, 2))
+        return c
+    lax.fori_loop(0, LAYERS * NG, fold, 0)
+    y = jnp.zeros((2 * LAYERS * HEADS, PAY), F32)
+    for xb in range(WIN):
+        hi, lo, _ = split3(folded[:, xb, :])
+        y = y + nt(jnp.concatenate([hi, lo], axis=0), fold_matrix(places[...], xb))
+    y = y[:LAYERS * HEADS] + y[LAYERS * HEADS:]
+    for l in range(LAYERS):
+        for t in range(2):
+            sums[l, t, :12, :PAY] = y[l * HEADS + t * 12:l * HEADS + t * 12 + 12]
+
     def small_copy(n, src, dst, device):
         return pltpu.make_async_remote_copy(src_ref=src, dst_ref=dst, send_sem=ssend.at[n], recv_sem=srecv.at[n],
                                             device_id=device, device_id_type=MESH)
     c = at.c
     core_swap = small_copy(0, sums.at[1 - c], sm_core, at.sibling())
     core_swap.start()
-    base = LAYERS * VIRT
+    base = base + LAYERS * NG // 2
     rs.tick(base)
     core_swap.wait_recv()
     for n in range(3):
@@ -784,19 +814,19 @@
     y_swap.start()
     rs.tick(base + 2)
     y_swap.wait_recv()
-    sm_z[at.z] = sm_y[0] + sm_y[1]
+    sm_z[at.z] = (sm_y[0] + sm_y[1]).astype(BF)
     z_swaps = [small_copy(3 + k, sm_z.at[at.z], sm_z.at[at.z], at.above(k)) for k in (1, 2, 3)]
     for cp in z_swaps:
         cp.start()
     rs.tick(base + 3)
     for cp in z_swaps:
         cp.wait_recv()
-    small[c] = (sm_z[0] + sm_z[1]) + (sm_z[2] + sm_z[3])
+    small[c] = (sm_z[0].astype(F32) + sm_z[1].astype(F32)) + (sm_z[2].astype(F32) + sm_z[3].astype(F32))
     last = small_copy(7, small.at[c], small.at[c], at.sibling())
     last.start()
     grad_swap.wait()
     gt[1 - t_here] = gin[...].astype(F32)
-    for n in range(4, REDUCE_LAGS[-1]):
+    for n in range(4, REDUCE_LAGS[-1] - LAYERS * NG // 2):
         rs.tick(base + n)
     last.wait()
     for cp in [core_swap, y_swap] + x_swaps + z_swaps:
@@ -810,24 +840,25 @@
     permt = jnp.asarray(perm.transpose(0, 2, 1), BF)
     return pl.pallas_call(
         backward_kernel,
-        out_shape=[sds((2, HALF, D), F32), sds((2, HALF, D), BF), sds((LAYERS * VIRT, 48, UC), F32),
+        out_shape=[sds((2, HALF, D), F32), sds((2, HALF, D), BF), sds((LAYERS * NU, 48, UC), F32),
                    sds((LAYERS, 2, 16, D), F32)],
         in_specs=[VM, SM, VM, VM, VM, VM, AN, AN] + [AN] * 8,
         out_specs=[VM, AN, VM, VM],
         scratch_shapes=[
-            pltpu.VMEM((TOK, D), F32), pltpu.VMEM((LAYERS, 3, 16, D), F32), pltpu.VMEM((HEADS, WIN, UC), F32),
-            pltpu.VMEM((HEADS, WT, UC), F32), pltpu.VMEM((3, 16, D), F32), pltpu.VMEM((2, 16, D), F32),
-            pltpu.VMEM((2, 2, 16, D), F32), pltpu.VMEM((4, 2, 16, D), F32), pltpu.VMEM((HALF, D), BF),
-            pltpu.VMEM((2, 2, 4, 2, 2, 48, UC), BF),
+            pltpu.VMEM((TOK, D), F32), pltpu.VMEM((WT, HT), F32), pltpu.VMEM((WT, HT), BF),
+            pltpu.VMEM((LAYERS, 3, 16, D), F32), pltpu.VMEM((LAYERS * HEADS, WIN, UC), F32),
+            pltpu.VMEM((LAYERS, NG, WT, HT), F32), pltpu.VMEM((3, 16, D), F32), pltpu.VMEM((2, 16, D), F32),
+            pltpu.VMEM((2, 2, 16, D), F32), pltpu.VMEM((4, 2, 16, D), BF), pltpu.VMEM((HALF, D), BF),
+            pltpu.VMEM((2, 4, 2, 2, 48, 2 * UC), BF),
             pltpu.VMEM((2, TOK, D), F32), pltpu.VMEM((TOK, D), BF), pltpu.VMEM((TOK, D), BF),
             pltpu.VMEM((3, TOK, D), BF), pltpu.VMEM((TOK, D), BF), pltpu.VMEM((TOK, D), BF),
             pltpu.VMEM((3, TOK, D), BF), pltpu.VMEM((TOK, D), F32), pltpu.VMEM((TOK, D), BF),
-            pltpu.VMEM((D, TOK), BF), pltpu.VMEM((D, TOK), BF), pltpu.VMEM((2, HG, WT, WT), BF),
-            pltpu.VMEM((2, 2, TOK, UC), BF), pltpu.VMEM((TOK, UC), F32), pltpu.VMEM((2, TOK, UC), BF),
-            pltpu.VMEM((REDUCE_SLOTS, 2, 4, 2, 2, 48, UC), BF),
-            pltpu.VMEM((REDUCE_SLOTS, 2, 4, 2, 48, UC), BF), pltpu.VMEM((REDUCE_SLOTS, 2, 4, 48, UC), BF),
+            pltpu.VMEM((D, TOK), BF), pltpu.VMEM((D, TOK), BF), pltpu.VMEM((2, WT, HT), BF),
+            pltpu.VMEM((2, 2, TOK, 2 * UC), BF), pltpu.VMEM((TOK, 2 * UC), F32), pltpu.VMEM((TOK, 2 * UC), BF),
+            pltpu.VMEM((REDUCE_SLOTS + CORE_SLOTS, 2, 4, 2, 48, UC), BF),
+            pltpu.VMEM((CORE_SLOTS, 2, 4, 2, 48, UC), BF), pltpu.VMEM((REDUCE_SLOTS, 2, 4, 48, UC), BF),
             pltpu.VMEM((REDUCE_SLOTS, 4, 48, UC), BF), pltpu.VMEM((REDUCE_SLOTS, 3, 48, UC), BF),
-            pltpu.SemaphoreType.DMA((2,)), pltpu.SemaphoreType.DMA((6,)),
+            pltpu.SemaphoreType.DMA((2, 2)), pltpu.SemaphoreType.DMA((6,)),
             pltpu.SemaphoreType.DMA((2,)), pltpu.SemaphoreType.DMA((2,)),
             pltpu.SemaphoreType.DMA((REDUCE_SLOTS, 7)), pltpu.SemaphoreType.DMA((REDUCE_SLOTS, 7)),
             pltpu.SemaphoreType.DMA((2,)), pltpu.SemaphoreType.DMA((2,)), pltpu.SemaphoreType.DMA((1,)),
@@ -1207,9 +1238,8 @@
 
 def unit_split(units):
     rows = units.shape[1]
-    units = units.reshape(LAYERS, VIRT, rows, UC)[::-1]
-    back = [p if p < GAP[0] else p + GAP[1] - GAP[0] for p in range(NU)]
-    units = jnp.stack([units[:, back[BACK_ORDER.index(u)]] for u in range(NU)], axis=1)
+    units = units.reshape(LAYERS, NU, rows, UC)[::-1]
+    units = jnp.stack([units[:, BACK_ORDER.index(u)] for u in range(NU)], axis=1)
     qkv = jnp.transpose(units[:, :3], (0, 2, 1, 3))
     proj = jnp.swapaxes(units[:, 3], 1, 2)
     ff = units[:, 4:].reshape(LAYERS, 4, 2, rows, UC)

time: 535 us -> 407 us (0.76)
  Pallas kernels: 506 us -> 378 us
    pallas_call x1, Pallas kernels: 287 us -> 204 us  [backward_call(): pl.pallas_call(backward_kernel, out_shape=[sds((2, HALF, D), F32), sds((2...]
    pallas_call x1, Pallas kernels: 219 us -> 174 us  [forward_call(): pl.pallas_call(forward_kernel, out_shape=[sds((TOK, D), BF), sds((16, D),...]
where the time goes in v2:
time: 407 us; the launch traced here: 402 us
  Pallas kernels  378 us (93%)
  local copies, waits for them, and re-layouts  19.8 us (5%)
    pallas_call x1, Pallas kernels, backward_call(): pl.pallas_call(backward_kernel, out_shape=[sds((2, HALF, D), F32), sds((2...  204 us
    pallas_call x1, Pallas kernels, forward_call(): pl.pallas_call(forward_kernel, out_shape=[sds((TOK, D), BF), sds((16, D),...  174 us
    unnamed x31, local copies, waits for them, and re-layouts  8.83 us

profile of v2, /device:TPU:0, one launch (start us, length us, event | category | flops | bytes accessed | tf_op | source)
XLA Modules:
  0.0 402.5 jit_solution(3152456742276322736)
XLA Ops:
  0.6 0.0 copy-start.4
  0.7 1.3 dynamic_slice.8.valid
  1.9 0.7 reshape.63
  2.6 0.7 pad_maximum_fusion.2
  3.4 0.7 reshape.64
  4.1 0.1 copy.44
  4.2 0.6 pad_bitcast_fusion.vshard
  4.8 0.8 copy.45
  5.7 0.7 select_maximum_fusion.pay
  6.3 1.0 reshape.66
  7.4 0.0 copy-done.4
  7.4 0.1 reshape.67
  7.4 0.0 copy-start.5
  7.5 0.0 copy-start.7
  7.5 0.4 pad_maximum_fusion.1
  7.9 0.1 copy.46
  8.0 0.0 copy-start.2
  8.0 0.0 copy-start.3
  8.0 0.4 copy-done.5
  8.4 0.1 copy-done.7
  8.4 1.0 pad_maximum_fusion
  9.5 0.0 copy-done.2
  9.5 0.0 copy-done.3
  9.5 1.4 copy_bitcast_fusion
  10.9 174.3 %forward.1 = (bf16[576,768]{1,0:T(8,128)(2,1)}, f32[16,768]{1,0:T(8,128)}, bf16[576,768]{1,0:T(8,128)(2,1)}, bf16[24,2,4,2,2,48,384]{6,5,4,3,2,1,0:T(8,128)(2,1)...) custom-call(bf16[2,288,768]{2,1,0:T(8,128)(2,1)} %get-tuple-element., ...), custom_call_target="tpu_custom_call" | custom-call | tf_op jit(solution)/shard_map/forward/pallas_call | solution.py:448
  185.2 203.5 %backward.1 = (f32[2,288,768]{2,1,0:T(8,128)}, bf16[2,288,768]{2,1,0:T(8,128)(2,1)}, f32[24,48,384]{2,1,0:T(8,128)}, f32[2,2,16,768]{3,2,1,0:T(8,128)}) custom-call(bf16[576,768]{1,0:T(8,128)(2,1)} %get-tuple-element.27.cot, s32[1]{0:T(128)} %dynamic_slice.8.valid, f32[16,768]{1,0:T(8,128)} %get-tuple-element.28.vec, s32[1,384]{1,0:T(1,128)} %constant.32.clone.places, ...), custom_call_target="tpu_custom_call" | custom-call | tf_op jit(solution)/shard_map/backward/pallas_call | solution.py:841
  388.8 0.0 copy-start.1
  388.8 3.1 copy.51
  391.9 0.0 copy-done.1
  391.9 0.0 copy-start.6
  391.9 0.0 copy-start
  391.9 2.6 copy.52
  394.5 0.0 copy-done.6
  394.5 0.1 dynamic-slice_bitcast_fusion
  394.6 0.6 slice.136
  395.1 0.6 slice.137
  395.7 0.6 slice.141
  396.4 0.7 copy.53
  397.0 0.6 copy.57
  397.6 0.0 copy-done
  397.6 0.1 fusion.7
  397.8 0.7 reverse_bitcast_fusion
  398.5 0.8 maximum_bitcast_fusion
  399.5 0.1 fusion.8
  399.5 0.2 copy.62
  399.8 1.1 reshape.74
  400.8 0.2 copy.63
  401.1 1.1 reshape.72
  (17 shorter events, 0.2 us)
Async XLA Ops:
  0.6 6.7 %copy-start.4 = (bf16[2,1536,48]{1,2,0:T(8,128)(2,1)S(1)}, bf16[2,1536,48]{1,2,0:T(8,128)(2,1)}, u32[]{:S(2)}) copy-start(bf16[2,1536,48]{1,2,0:T(8,128)(2,1)} %param.29) | copy-start | bytes 884740
  7.4 0.9 copy-start.5
  7.5 1.0 copy-start.7
  8.0 1.5 copy-start.2
  8.0 1.5 copy-start.3
  388.8 3.1 copy-start.1
  391.9 2.6 copy-start.6
  391.9 5.7 %copy-start = (f32[24,48,384]{2,1,0:T(8,128)S(1)}, f32[24,48,384]{2,1,0:T(8,128)}, u32[]{:S(2)}) copy-start(f32[24,48,384]{2,1,0:T(8,128)} %get-tuple-element.42) | copy-start | bytes 5308420

commit v3 on v2

--- a/solution.py
+++ b/solution.py
@@ -141,7 +141,7 @@
 MESH = pl.DeviceIdType.MESH
 GATHER_LAGS = (2, 4, 6, 7)
 GATHER_SEMS = 12
-TICK_EVERY = 6
+TICK_EVERY = (12, 6)
 
 
 class Gather:
@@ -277,8 +277,32 @@
     for n in range(2):
         swaps[n].start()
         keeps[n].start()
+    def both(row):
+        return jnp.concatenate([pays[0, pl.ds(row, 1), :UC], pays[1, pl.ds(row, 1), :UC]], axis=1)
+
+    def vrow(l, i):
+        return vec[pl.ds(l * 6 + i, 1)]
+
+    def spread(i, c):
+        half, l, g = lax.div(i, 6), lax.rem(lax.div(i, 3), 2), lax.rem(i, 3)
+        for h in range(HG):
+            x = ext[half * 24 + l * 12 + g * HG + h]
+            for yb in range(WIN):
+                off = (WIN - 1 - yb) * WIN
+                bias[l, half * 3 + g, yb * WIN:(yb + 1) * WIN, h * WT:(h + 1) * WT] = x[:, off:off + WT]
+        return c
+
+    def norm_first(l):
+        def ln1(i):
+            r = pl.ds(i * WT, WT)
+            xh, _ = norm_parts(x0[l, r])
+            ow[l, r] = (xh * vrow(l, 0) + vrow(l, 2)).astype(BF)
+        rows_loop(4, ln1)
+        n1[l] = nn(perm[l], ow[l]).astype(BF)
+
     for n in range(lag + 1):
-        vg.tick(n)
+        if n < 5:
+            vg.stage(n, 0)
         ag.tick(n)
         if n == 0:
             swaps[1].wait()
@@ -288,60 +312,56 @@
             for xa in range(WIN):
                 y = nn(parts, fold_matrix(places[...], xa))
                 ext[:, xa, :] = y[:48] + y[48:96] + y[96:]
-    def spread(i, c):
-        half, l, g = lax.div(i, 6), lax.rem(lax.div(i, 3), 2), lax.rem(i, 3)
-        for h in range(HG):
-            x = ext[half * 24 + l * 12 + g * HG + h]
-            for yb in range(WIN):
-                off = (WIN - 1 - yb) * WIN
-                bias[l, half * 3 + g, yb * WIN:(yb + 1) * WIN, h * WT:(h + 1) * WT] = x[:, off:off + WT]
-        return c
-    lax.fori_loop(0, 12, spread, 0)
-    vec[...] = vall[0, 0].reshape(D, 128).astype(F32).T[:16]
-    swaps[0].wait()
-    keeps[0].wait()
-
-    def both(row):
-        return jnp.concatenate([pays[0, pl.ds(row, 1), :UC], pays[1, pl.ds(row, 1), :UC]], axis=1)
-
-    def vrow(l, i):
-        return vec[pl.ds(l * 6 + i, 1)]
+        if n == 2:
+            lax.fori_loop(0, 6, spread, 0)
+        if n == 3:
+            lax.fori_loop(6, 12, spread, 0)
+        if n == 4:
+            vec[...] = vall[0, 0].reshape(D, 128).astype(F32).T[:16]
+            swaps[0].wait()
+            keeps[0].wait()
+            x0[0] = xin[...].astype(F32)
+        if n == 5:
+            norm_first(0)
 
     def fetch(g, u):
         return Fetch(w_hbm, wbuf, wsem, g, u % 2)
 
     def tick_base(l, u):
-        inside = 4 * NG // TICK_EVERY
-        return lag + 1 + l * (NU + inside) + u + (inside if u > 3 else 0)
+        before, inside = (4 * NG // every for every in TICK_EVERY)
+        return lag + 1 + l * (NU + before) + u + (jnp.where(l == 0, before, inside) if u >= 3 else 0)
 
     def step_unit(l, u):
         g = l * NU + u
         fetch(g, u).wait()
-        ag.tick(tick_base(l, u) + (4 * NG // TICK_EVERY if u == 3 else 0))
+        ag.tick(tick_base(l, u))
 
         @pl.when(g + 1 < LAYERS * NU)
         def _():
             fetch(g + 1, u + 1).start()
 
     fetch(0, 0).start()
-    x0[0] = xin[...].astype(F32)
     lanes = lax.shift_right_logical(lax.broadcasted_iota(jnp.int32, (WT, HG * HDIM), 1), 5)
+
+    kept = ((x0, x0_h), (x1, x1_h), (n1, n1_h), (qkv, qkv_h), (ow, o_h), (n2, n2_h))
+
+    def save(l, *which):
+        for n in which:
+            pltpu.make_async_copy(kept[n][0].at[l], kept[n][1].at[l], ssem.at[l]).start()
 
     def layer(l, carry):
         x0_l, x1_l, n1_l, n2_l, ow_l = x0.at[l], x1.at[l], n1.at[l], n2.at[l], ow.at[l]
 
-        def ln1(i):
-            r = pl.ds(i * WT, WT)
-            xh, _ = norm_parts(x0_l[r])
-            ow_l[r] = (xh * vrow(l, 0) + vrow(l, 2)).astype(BF)
-        rows_loop(4, ln1)
-        n1_l[...] = nn(perm[l], ow_l[...]).astype(BF)
+        @pl.when(l > 0)
+        def _():
+            norm_first(l)
         for j in range(3):
             step_unit(l, j)
             y = nn(n1_l[...], w2d(wbuf, j % 2))
             if j != 1:
                 y = y + both(l * 2 + j // 2)
             qkv[l, j] = y.astype(BF)
+        save(l, 0, 2, 3)
 
         def attend(it, c):
             w, hg = lax.div(it, NG), lax.rem(it, NG)
@@ -362,11 +382,15 @@
             ow_l[r, cl] = own_blocks(nn(v.T, pst[slot])).astype(BF)
             put.start()
 
-            @pl.when(lax.rem(it, TICK_EVERY) == TICK_EVERY - 1)
+            every = jnp.where(l == 0, TICK_EVERY[0], TICK_EVERY[1])
+
+            @pl.when(lax.rem(it, every) == every - 1)
             def _():
-                ag.tick(tick_base(l, 3) + lax.div(it, TICK_EVERY))
+                ag.tick(tick_base(l, 2) + 1 + lax.div(it, every))
             return c
         lax.fori_loop(0, 4 * NG, attend, 0)
+
+        save(l, 4)
 
         @pl.when(l == LAYERS - 1)
         def _():
@@ -384,6 +408,7 @@
             n2_l[r] = (xh * vrow(l, 1) + vrow(l, 4)).astype(BF)
             acc[r] = x + vrow(l, 5)
         rows_loop(4, ln2)
+        save(l, 1, 5)
         for i in range(4):
             step_unit(l, 4 + 2 * i)
             put = pltpu.make_async_copy(gst.at[i % 2], gg_h.at[l, i], gsem.at[i % 2])
@@ -405,20 +430,17 @@
             step_unit(l, 5 + 2 * i)
             acc[...] += nt(gst[i % 2, 0], w2d(wbuf, 1))
 
-        for ref, dst in ((x0, x0_h), (x1, x1_h), (n1, n1_h), (qkv, qkv_h), (ow, o_h), (n2, n2_h)):
-            pltpu.make_async_copy(ref.at[l], dst.at[l], ssem.at[l]).start()
-
         @pl.when(l == 0)
         def _():
             x0[1] = acc[...]
 
         @pl.when(l == 1)
         def _():
-            out[...] = (acc[...] * valid[0].astype(F32)).astype(BF)
+            out[...] = (acc[...] * valid[at.t].astype(F32)).astype(BF)
         return carry
     lax.fori_loop(0, LAYERS, layer, 0)
     for l in range(LAYERS):
-        for ref, dst in ((x0, x0_h), (x1, x1_h), (n1, n1_h), (qkv, qkv_h), (ow, o_h), (n2, n2_h)):
+        for ref, dst in kept:
             pltpu.make_async_copy(ref.at[l], dst.at[l], ssem.at[l]).wait()
     for s in range(2):
         pltpu.make_async_copy(pst.at[s], pw_h.at[0, 0, 0], psem.at[s]).wait()
@@ -488,9 +510,9 @@
 CORE_SLOTS = 4
 PAY = 640
 HALF = TOK // 2
-VIRT = 18
-GAP = (9, 15)
-REDUCE_LAGS = (1, 5, 8, 11)
+VIRT = 16
+GAP = (9, 13)
+REDUCE_LAGS = (1, 6, 10, 14)
 
 
 class Reduce:
@@ -571,7 +593,9 @@
             for k in (1, 2, 3):
                 self.up(v, k).wait_recv()
                 total = total + self.z_in[slot, k - 1].astype(F32)
-            self.total[lax.div(v, VIRT) * NU + slot] = total
+            ff = jnp.where(lax.rem(slot, 2) == 0, 8, 4) + lax.div(slot, 2)
+            unit = jnp.where(slot < 8, ff, jnp.where(slot == 8, 3, slot - 9))
+            self.total[LAYERS - 1 - lax.div(v, VIRT), unit] = total
             for n in range(2):
                 self.first(v, n).wait_send()
             self.second(v).wait_send()
@@ -628,15 +652,15 @@
     block_swap.start()
     block_keep.start()
     total[...] = jnp.zeros_like(total)
-    e[...] = cot[...].astype(F32) * valid[0].astype(F32)
+    e[...] = cot[...].astype(F32) * valid[at.t].astype(F32)
     sums[...] = jnp.zeros_like(sums)
     lanes = lax.shift_right_logical(lax.broadcasted_iota(jnp.int32, (WT, HG * HDIM), 1), 5)
 
     def layer(step, carry):
         l = LAYERS - 1 - step
         loads = [pltpu.make_async_copy(src.at[l], dst, lsem.at[n]) for n, (src, dst) in enumerate((
-            (n2_h, n2), (x1_h, xb.at[1]), (o_h, ow), (qkv_h, qkv), (n1_h, n1), (x0_h, xb.at[0])))]
-        for cp in loads:
+            (n2_h, n2), (x1_h, xb), (o_h, ow), (qkv_h, qkv), (n1_h, n1), (x0_h, xb)))]
+        for cp in loads[:5]:
             cp.start()
 
         def load_gg(k):
@@ -680,7 +704,7 @@
 
         def ln2(i):
             r = pl.ds(i * WT, WT)
-            grad, gsum, bsum = norm_back(xb[1, r], acc[r], vec[pl.ds(l * 6 + 1, 1)])
+            grad, gsum, bsum = norm_back(xb[r], acc[r], vec[pl.ds(l * 6 + 1, 1)])
             x = e[r] + grad
             e[r] = x
             em[r] = x.astype(BF)
@@ -688,6 +712,7 @@
             sums[l, 2, 4:5] += bsum
             sums[l, 2, 3:4] += jnp.sum(x, axis=0, keepdims=True)
         rows_loop(4, ln2)
+        loads[5].start()
         n2[...] = nn(perm[l], em[...]).astype(BF)
         emt[...] = n2[...].T
         step_unit(l, 8)
@@ -726,9 +751,9 @@
             dqkv[1, r, cl] = (nn(ds[...], q4) * SCALE).astype(BF)
             dqkv[2, r, cl] = nn(pst[slot], d4).astype(BF)
 
-            @pl.when(lax.rem(it, 4) == 3)
+            @pl.when(lax.rem(it, 6) == 5)
             def _():
-                rs.tick(step * VIRT + GAP[0] + lax.div(it, 4))
+                rs.tick(step * VIRT + GAP[0] + lax.div(it, 6))
             return c
         lax.fori_loop(0, 4 * NG, attend, 0)
 
@@ -739,19 +764,20 @@
         loads[4].wait()
         emt[...] = n1[...].T
         for j in range(3):
+            emit(l, 9 + j, nn(emt[...], dqkv[j]))
+        for j in range(3):
             step_unit(l, 9 + j)
             y = nt(dqkv[j], w2d(wbuf, (9 + j) % 2))
             if j == 0:
                 acc[...] = y
             else:
                 acc[...] += y
-            emit(l, 9 + j, nn(emt[...], dqkv[j]))
         acc[...] = nn(permt[l], acc[...].astype(BF))
         loads[5].wait()
 
         def ln1(i):
             r = pl.ds(i * WT, WT)
-            grad, gsum, bsum = norm_back(xb[0, r], acc[r], vec[pl.ds(l * 6, 1)])
+            grad, gsum, bsum = norm_back(xb[r], acc[r], vec[pl.ds(l * 6, 1)])
             e[r] += grad
             sums[l, 2, 0:1] += gsum
             sums[l, 2, 2:3] += bsum
@@ -840,7 +866,7 @@
     permt = jnp.asarray(perm.transpose(0, 2, 1), BF)
     return pl.pallas_call(
         backward_kernel,
-        out_shape=[sds((2, HALF, D), F32), sds((2, HALF, D), BF), sds((LAYERS * NU, 48, UC), F32),
+        out_shape=[sds((2, HALF, D), F32), sds((2, HALF, D), BF), sds((LAYERS, NU, 48, UC), F32),
                    sds((LAYERS, 2, 16, D), F32)],
         in_specs=[VM, SM, VM, VM, VM, VM, AN, AN] + [AN] * 8,
         out_specs=[VM, AN, VM, VM],
@@ -850,7 +876,7 @@
             pltpu.VMEM((LAYERS, NG, WT, HT), F32), pltpu.VMEM((3, 16, D), F32), pltpu.VMEM((2, 16, D), F32),
             pltpu.VMEM((2, 2, 16, D), F32), pltpu.VMEM((4, 2, 16, D), BF), pltpu.VMEM((HALF, D), BF),
             pltpu.VMEM((2, 4, 2, 2, 48, 2 * UC), BF),
-            pltpu.VMEM((2, TOK, D), F32), pltpu.VMEM((TOK, D), BF), pltpu.VMEM((TOK, D), BF),
+            pltpu.VMEM((TOK, D), F32), pltpu.VMEM((TOK, D), BF), pltpu.VMEM((TOK, D), BF),
             pltpu.VMEM((3, TOK, D), BF), pltpu.VMEM((TOK, D), BF), pltpu.VMEM((TOK, D), BF),
             pltpu.VMEM((3, TOK, D), BF), pltpu.VMEM((TOK, D), F32), pltpu.VMEM((TOK, D), BF),
             pltpu.VMEM((D, TOK), BF), pltpu.VMEM((D, TOK), BF), pltpu.VMEM((2, WT, HT), BF),
@@ -1237,20 +1263,16 @@
 
 
 def unit_split(units):
-    rows = units.shape[1]
-    units = units.reshape(LAYERS, NU, rows, UC)[::-1]
-    units = jnp.stack([units[:, BACK_ORDER.index(u)] for u in range(NU)], axis=1)
+    rows = units.shape[2]
     qkv = jnp.transpose(units[:, :3], (0, 2, 1, 3))
     proj = jnp.swapaxes(units[:, 3], 1, 2)
-    ff = units[:, 4:].reshape(LAYERS, 4, 2, rows, UC)
-    fc1 = jnp.transpose(ff[:, :, 0], (0, 2, 1, 3)).reshape(LAYERS, rows, 4 * UC)
-    fc2 = jnp.transpose(ff[:, :, 1], (0, 1, 3, 2)).reshape(LAYERS, 4 * UC, rows)
+    fc1 = jnp.transpose(units[:, 4:8], (0, 2, 1, 3)).reshape(LAYERS, rows, 4 * UC)
+    fc2 = jnp.transpose(units[:, 8:], (0, 1, 3, 2)).reshape(LAYERS, 4 * UC, rows)
     return qkv, proj, fc1, fc2
 
 
 def image_shards(tokens, valid, cotangent, row_gain, row_bias, w_qkv, qv_bias, w_proj, w_fc1, fc1_bias, w_fc2, rel_table):
-    t, d = lax.axis_index("tensor"), lax.axis_index("dp")
-    here = lax.dynamic_slice(valid, (t,), (1,))
+    d = lax.axis_index("dp")
     shard = unit_stack(w_qkv, w_proj, w_fc1, w_fc2)
     vecs = jnp.concatenate([row_gain, row_bias], axis=1).reshape(LAYERS * 6, 48)
     vshard = jnp.pad(vecs.T, ((0, 0), (0, 128 - LAYERS * 6)))[None]
@@ -1258,8 +1280,8 @@
     pay = jnp.concatenate([jnp.pad(rows, ((0, 4), (0, PAY - UC))),
                            jnp.pad(rel_table.reshape(LAYERS * 12, RELS), ((0, 0), (0, PAY - RELS)))])
     block, vec, cot, w, *saved = forward_call(
-        jnp.swapaxes(tokens, 0, 1), jnp.swapaxes(cotangent, 0, 1), here, vshard, pay, shard)
-    gt, block, total, small = backward_call(cot, here, vec, block, w, *saved)
+        jnp.swapaxes(tokens, 0, 1), jnp.swapaxes(cotangent, 0, 1), valid, vshard, pay, shard)
+    gt, block, total, small = backward_call(cot, valid, vec, block, w, *saved)
     qkv_g, proj_g, fc1_g, fc2_g = unit_split(total)
     rowg = lax.dynamic_slice(small[:, 1], (0, 0, d * 48), (LAYERS, 6, 48))
     own = small[:, 0]

time: 407 us -> 385 us (0.946)
  Pallas kernels: 378 us -> 358 us
    pallas_call x1, Pallas kernels: 204 us -> 189 us  [backward_call(): pl.pallas_call(backward_kernel, out_shape=[sds((2, HALF, D), F32), sds((2...]
    pallas_call x1, Pallas kernels: 174 us -> 169 us  [forward_call(): pl.pallas_call(forward_kernel, out_shape=[sds((TOK, D), BF), sds((16, D),...]
where the time goes in v3:
time: 385 us; the launch traced here: 379 us
  Pallas kernels  358 us (93%)
  local copies, waits for them, and re-layouts  18.2 us (5%)
    pallas_call x1, Pallas kernels, backward_call(): pl.pallas_call(backward_kernel, out_shape=[sds((2, HALF, D), F32), sds((2...  189 us
    pallas_call x1, Pallas kernels, forward_call(): pl.pallas_call(forward_kernel, out_shape=[sds((TOK, D), BF), sds((16, D),...  169 us

profile of v3, /device:TPU:0, one launch (start us, length us, event | category | flops | bytes accessed | tf_op | source)
XLA Modules:
  0.0 379.4 jit_solution(13858695022650111970)
XLA Ops:
  0.6 0.0 copy-start.2
  0.7 0.0 copy-start.3
  0.7 2.9 copy_bitcast_fusion
  3.6 0.0 copy-done.2
  3.6 0.0 copy-start.4
  3.6 0.0 copy-start.6
  3.6 0.1 reshape.61
  3.7 0.0 copy-done.3
  3.7 0.1 reshape.60
  3.8 0.4 pad_maximum_fusion.1
  4.2 0.0 copy-start.7
  4.2 0.0 copy-start.8
  4.2 0.0 copy-start.9
  4.2 0.0 copy-start.10
  4.2 0.0 copy-start.11
  4.2 0.1 copy.43
  4.3 0.2 copy-done.4
  4.5 0.1 copy-done.6
  4.6 1.0 pad_maximum_fusion
  5.6 0.0 copy-done.7
  5.7 0.0 copy-done.8
  5.7 0.0 copy-done.9
  5.7 0.7 select_maximum_fusion.pay
  6.4 0.0 copy-done.10
  6.4 0.0 copy-done.11
  6.4 0.1 copy.41
  6.5 0.6 pad_bitcast_fusion.vshard
  7.1 169.1 %forward.1 = (bf16[576,768]{1,0:T(8,128)(2,1)}, f32[16,768]{1,0:T(8,128)}, bf16[576,768]{1,0:T(8,128)(2,1)}, bf16[24,2,4,2,2,48,384]{6,5,4,3,2,1,0:T(8,128)(2,1)...) custom-call(bf16[2,288,768]{2,1,0:T(8,128)(2,1)} %get-tuple-element., ...), custom_call_target="tpu_custom_call" | custom-call | tf_op jit(solution)/shard_map/forward/pallas_call | solution.py:470
  176.2 188.8 %backward.1 = (f32[2,288,768]{2,1,0:T(8,128)}, bf16[2,288,768]{2,1,0:T(8,128)(2,1)}, f32[2,12,48,384]{3,2,1,0:T(8,128)}, f32[2,2,16,768]{3,2,1,0:T(8,128)}) custom-call(bf16[576,768]{1,0:T(8,128)(2,1)} %get-tuple-element.27.cot, s32[2]{0:T(128)} %valid.3, f32[16,768]{1,0:T(8,128)} %get-tuple-element.28.vec, s32[1,384]{1,0:T(1,128)} %constant.28.clone.places, ...), custom_call_target="tpu_custom_call" | custom-call | tf_op jit(solution)/shard_map/backward/pallas_call | solution.py:867
  365.0 1.3 slice_bitcast_fusion
  366.3 0.0 copy-start
  366.4 0.9 copy.50
  367.2 0.9 copy.51
  368.1 0.0 copy-done
  368.1 0.0 copy-start.1
  368.1 2.6 copy.48
  370.7 0.0 copy-start.5
  370.7 0.0 copy-done.1
  370.7 1.8 copy.47
  372.5 1.8 slice_bitcast_fusion.2
  374.3 0.0 copy-done.5
  374.3 0.7 copy.49
  375.0 0.6 copy.52
  375.6 0.1 dynamic-slice_bitcast_fusion
  375.7 0.6 slice.45
  376.3 0.6 slice.44
  376.9 0.6 slice.46
  377.5 1.6 slice_bitcast_fusion.3
  (10 shorter events, 0.1 us)
Async XLA Ops:
  0.6 2.9 copy-start.2
  0.7 3.0 copy-start.3
  3.6 0.9 copy-start.4
  3.6 1.0 copy-start.6
  4.2 1.4 copy-start.7
  4.2 1.5 copy-start.8
  4.2 1.5 copy-start.9
  4.2 2.2 copy-start.10
  4.2 2.1 copy-start.11
  366.3 1.8 copy-start
  368.1 2.6 copy-start.1
  370.7 3.6 copy-start.5

commit v4 on v3

--- a/solution.py
+++ b/solution.py
@@ -824,6 +824,7 @@
     core_swap.start()
     base = base + LAYERS * NG // 2
     rs.tick(base)
+    rs.tick(base + 1)
     core_swap.wait_recv()
     for n in range(3):
         sums[c, n] += sm_core[n]
@@ -831,20 +832,22 @@
                small_copy(2, sums.at[c, 2], sm_x.at[1], at.side(at.x_side))]
     for cp in x_swaps:
         cp.start()
-    rs.tick(base + 1)
+    rs.tick(base + 2)
+    rs.tick(base + 3)
     for cp in x_swaps:
         cp.wait_recv()
     sm_y[0, 0] = sums[c, t_here] + sm_x[0]
     sm_y[0, 1] = sums[c, 2] + sm_x[1]
     y_swap = small_copy(3, sm_y.at[0], sm_y.at[1], at.side(at.y_side))
     y_swap.start()
-    rs.tick(base + 2)
+    rs.tick(base + 4)
+    rs.tick(base + 5)
     y_swap.wait_recv()
     sm_z[at.z] = (sm_y[0] + sm_y[1]).astype(BF)
     z_swaps = [small_copy(3 + k, sm_z.at[at.z], sm_z.at[at.z], at.above(k)) for k in (1, 2, 3)]
     for cp in z_swaps:
         cp.start()
-    rs.tick(base + 3)
+    rs.tick(base + 6)
     for cp in z_swaps:
         cp.wait_recv()
     small[c] = (sm_z[0].astype(F32) + sm_z[1].astype(F32)) + (sm_z[2].astype(F32) + sm_z[3].astype(F32))
@@ -852,7 +855,7 @@
     last.start()
     grad_swap.wait()
     gt[1 - t_here] = gin[...].astype(F32)
-    for n in range(4, REDUCE_LAGS[-1] - LAYERS * NG // 2):
+    for n in range(7, REDUCE_LAGS[-1] - LAYERS * NG // 2):
         rs.tick(base + n)
     last.wait()
     for cp in [core_swap, y_swap] + x_swaps + z_swaps:

time: 385 us -> 383 us (level)
  no operation moved by 1% of the time
where the time goes in v4:
time: 383 us; the launch traced here: 378 us
  Pallas kernels  357 us (93%)
  local copies, waits for them, and re-layouts  18.2 us (5%)
    pallas_call x1, Pallas kernels, backward_call(): pl.pallas_call(backward_kernel, out_shape=[sds((2, HALF, D), F32), sds((2...  188 us
    pallas_call x1, Pallas kernels, forward_call(): pl.pallas_call(forward_kernel, out_shape=[sds((TOK, D), BF), sds((16, D),...  169 us

profile of v4, /device:TPU:0, one launch (start us, length us, event | category | flops | bytes accessed | tf_op | source)
XLA Modules:
  0.0 378.3 jit_solution(11399111443074552654)
XLA Ops:
  0.6 0.0 copy-start.2
  0.7 0.0 copy-start.3
  0.7 2.9 copy_bitcast_fusion
  3.6 0.0 copy-done.2
  3.6 0.0 copy-start.4
  3.6 0.0 copy-start.6
  3.6 0.1 reshape.61
  3.7 0.0 copy-done.3
  3.7 0.1 reshape.60
  3.8 0.4 pad_maximum_fusion.1
  4.2 0.0 copy-start.7
  4.2 0.0 copy-start.8
  4.2 0.0 copy-start.9
  4.2 0.0 copy-start.10
  4.2 0.0 copy-start.11
  4.2 0.1 copy.43
  4.3 0.2 copy-done.4
  4.5 0.1 copy-done.6
  4.6 1.0 pad_maximum_fusion
  5.6 0.0 copy-done.7
  5.7 0.0 copy-done.8
  5.7 0.0 copy-done.9
  5.7 0.7 select_maximum_fusion.pay
  6.4 0.0 copy-done.10
  6.4 0.0 copy-done.11
  6.4 0.1 copy.41
  6.5 0.6 pad_bitcast_fusion.vshard
  7.1 169.1 %forward.1 = (bf16[576,768]{1,0:T(8,128)(2,1)}, f32[16,768]{1,0:T(8,128)}, bf16[576,768]{1,0:T(8,128)(2,1)}, bf16[24,2,4,2,2,48,384]{6,5,4,3,2,1,0:T(8,128)(2,1)...) custom-call(bf16[2,288,768]{2,1,0:T(8,128)(2,1)} %get-tuple-element., ...), custom_call_target="tpu_custom_call" | custom-call | tf_op jit(solution)/shard_map/forward/pallas_call | solution.py:470
  176.2 187.6 %backward.1 = (f32[2,288,768]{2,1,0:T(8,128)}, bf16[2,288,768]{2,1,0:T(8,128)(2,1)}, f32[2,12,48,384]{3,2,1,0:T(8,128)}, f32[2,2,16,768]{3,2,1,0:T(8,128)}) custom-call(bf16[576,768]{1,0:T(8,128)(2,1)} %get-tuple-element.27.cot, s32[2]{0:T(128)} %valid.3, f32[16,768]{1,0:T(8,128)} %get-tuple-element.28.vec, s32[1,384]{1,0:T(1,128)} %constant.28.clone.places, ...), custom_call_target="tpu_custom_call" | custom-call | tf_op jit(solution)/shard_map/backward/pallas_call | solution.py:870
  363.8 1.3 slice_bitcast_fusion
  365.2 0.0 copy-start
  365.2 0.9 copy.50
  366.1 0.9 copy.51
  366.9 0.0 copy-done
  366.9 0.0 copy-start.1
  366.9 2.6 copy.48
  369.5 0.0 copy-start.5
  369.5 0.0 copy-done.1
  369.5 1.8 copy.47
  371.3 1.8 slice_bitcast_fusion.2
  373.2 0.0 copy-done.5
  373.2 0.7 copy.49
  373.9 0.6 copy.52
  374.5 0.1 dynamic-slice_bitcast_fusion
  374.5 0.6 slice.45
  375.1 0.6 slice.44
  375.7 0.6 slice.46
  376.3 1.6 slice_bitcast_fusion.3
  (10 shorter events, 0.1 us)
Async XLA Ops:
  0.6 2.9 copy-start.2
  0.7 3.0 copy-start.3
  3.6 0.9 copy-start.4
  3.6 1.0 copy-start.6
  4.2 1.4 copy-start.7
  4.2 1.5 copy-start.8
  4.2 1.5 copy-start.9
  4.2 2.2 copy-start.10
  4.2 2.1 copy-start.11
  365.2 1.8 copy-start
  366.9 2.6 copy-start.1
  369.5 3.6 copy-start.5
